TPU v7x, 32 devices: a whole 2x2x4 slice. The times are simulated.
32 devices in a mesh: seq: 4 (over z), fsdp: 8 (over y, x, core).
Axes of the slice: x: 2, y: 2, z: 4, core: 2. Of those that a mesh axis runs over, the one named last changes fastest.
Arguments:
- tokens: bfloat16 [8, 1024, 768], P('fsdp', 'seq'), may hold values from -6 to 6
- routes: int32 [8, 1024, 1], P('fsdp', 'seq'), may hold values from 0 to 1; in each aligned block of 256 rows (0 to 255, 256 to 511, ..., all dimensions but the last counted through in order) at most 144 rows name the same one
- buckets: int32 [2047], replicated, may hold values from 0 to 31
- gain_attn: float32 [768], replicated, may hold values from 0.1 to 1.9
- w_query: bfloat16 [768, 768], P('fsdp'), may hold values from -0.21875 to 0.21875
- w_key: bfloat16 [768, 768], P('fsdp'), may hold values from -0.21875 to 0.21875
- w_value: bfloat16 [768, 768], P('fsdp'), may hold values from -0.21875 to 0.21875
- w_out: bfloat16 [768, 768], P('fsdp'), may hold values from -3.5 to 3.5
- bias_table: float32 [32, 12], replicated, may hold values from -6 to 6
- gain_ff: float32 [768], replicated, may hold values from 0.1 to 1.9
- router: float32 [768, 2], replicated, may hold values from -0.15625 to 0.15625
- expert_up: bfloat16 [2, 3072, 768], P(None, ('seq', 'fsdp')), may hold values from -0.21875 to 0.21875
- expert_down: bfloat16 [2, 3072, 768], P(None, ('seq', 'fsdp')), may hold values from -0.3125 to 0.3125
- out_grad: bfloat16 [8, 1024, 768], P('fsdp', 'seq'), may hold values from -6 to 6
Outputs:
- output: bfloat16 [8, 1024, 768], P('fsdp', 'seq')
- tokens_grad: float32 [8, 1024, 768], P('fsdp', 'seq')
- gain_attn_grad: float32 [768], replicated
- w_query_grad: float32 [768, 768], P('fsdp')
- w_key_grad: float32 [768, 768], P('fsdp')
- w_value_grad: float32 [768, 768], P('fsdp')
- w_out_grad: float32 [768, 768], P('fsdp')
- bias_table_grad: float32 [32, 12], replicated
- gain_ff_grad: float32 [768], replicated
- router_grad: float32 [768, 2], replicated
- expert_up_grad: float32 [2, 3072, 768], P(None, ('seq', 'fsdp'))
- expert_down_grad: float32 [2, 3072, 768], P(None, ('seq', 'fsdp'))
Inputs may be any that keep to these rules, and one draw needn't show every extreme that they name: `routes`: in each aligned block of 256 positions of a sequence, at most 144 tokens name one expert.
All inputs are finite; a program needn't handle non-finite values.
Results may differ from a plain program's by a relative error of at most 0.017.
Values may be sent and summed in bfloat16 or wider, within the bound.
No kernel may reach another device: no remote copies, remote signals or barrier semaphores. Data moves between devices by JAX's collectives and lax.ppermute only.
A program may use at most 192 MiB of HBM per device.

v0:
```python
import jax
import jax.numpy as jnp
from jax import lax
from jax.sharding import PartitionSpec as P

HEAD = 64


EPSILON = 1e-06
PRECISE = lax.Precision.HIGHEST
ROOT_HALF = 0.7071067811865476
DENSITY = 0.3989422804014327


def gelu_slope(pre_act):
    normal_cdf = 0.5 * (1.0 + lax.erf(pre_act * ROOT_HALF))
    return (
        pre_act * normal_cdf,
        normal_cdf + pre_act * jnp.exp(-0.5 * pre_act * pre_act) * DENSITY,
    )


def norm_scale(values):
    return lax.rsqrt(jnp.mean(values * values, axis=-1, keepdims=True) + EPSILON)


def norm_back(values, scaled_by, gain, upstream):
    weighted = upstream * gain
    inner_sum = jnp.mean(weighted * values, axis=-1, keepdims=True)
    cubed = scaled_by * scaled_by * scaled_by
    return (
        scaled_by * weighted - values * cubed * inner_sum,
        jnp.sum(upstream * values * scaled_by, axis=(0, 1)),
    )


def bias_window(offset_bias, first_row, block_rows, length):
    head_count = offset_bias.shape[0]
    window_width = length + block_rows - 1
    window = lax.dynamic_slice_in_dim(offset_bias, length - block_rows - first_row, window_width, 1)
    padded = jnp.pad(window, ((0, 0), (0, 1)))
    tiled = jnp.broadcast_to(padded[:, None, :], (head_count, block_rows, window_width + 1))
    skewed = tiled.reshape(head_count, block_rows * (window_width + 1))[
        :, : block_rows * window_width
    ]
    return skewed.reshape(head_count, block_rows, window_width)[
        :, :, block_rows - 1 : block_rows - 1 + length
    ]


def bias_window_back(grad_scores, block_rows, length):
    head_count = grad_scores.shape[0]
    window_width = length + block_rows - 1
    placed = jnp.pad(grad_scores, ((0, 0), (0, 0), (block_rows - 1, 0)))
    flat_rows = jnp.pad(
        placed.reshape(head_count, block_rows * window_width), ((0, 0), (0, block_rows))
    )
    return jnp.sum(
        flat_rows.reshape(head_count, block_rows, window_width + 1), axis=1, dtype=jnp.float32
    )[:, :window_width]


def block_scores(query_rows, key_heads, bias_rows):
    raw_scores = jnp.einsum(
        "ihd,jhd->hij", query_rows, key_heads, preferred_element_type=jnp.float32
    )
    return raw_scores * HEAD ** (-0.5) + bias_rows


def attend_forward(query_seq, key_seq, value_seq, bias_blocks, block_rows):
    length, local_width = query_seq.shape
    head_count = local_width // HEAD
    block_count = length // block_rows
    query_blocks = query_seq.reshape(block_count, block_rows, head_count, HEAD)
    key_heads = key_seq.reshape(length, head_count, HEAD)
    value_heads = value_seq.reshape(length, head_count, HEAD)

    def one_block(block_pair):
        bias_rows, query_rows = block_pair
        scores = block_scores(query_rows, key_heads, bias_rows)
        row_max = jnp.max(scores, axis=-1, keepdims=True)
        shifted = jnp.exp(scores - row_max)
        row_total = jnp.sum(shifted, axis=-1, keepdims=True)
        weights = (shifted / row_total).astype(jnp.bfloat16)
        context = jnp.einsum(
            "hij,jhd->ihd", weights, value_heads, preferred_element_type=jnp.float32
        )
        return (
            context.astype(jnp.bfloat16).reshape(block_rows, local_width),
            (row_max + jnp.log(row_total))[:, :, 0],
        )

    contexts, log_totals = lax.map(one_block, (bias_blocks, query_blocks))
    return (contexts.reshape(length, local_width), log_totals)


def attend_backward(query_seq, key_seq, value_seq, grad_seq, log_totals, bias_blocks, block_rows):
    length, local_width = query_seq.shape
    head_count = local_width // HEAD
    block_count = length // block_rows
    window_width = length + block_rows - 1
    scale_factor = HEAD ** (-0.5)
    query_blocks = query_seq.reshape(block_count, block_rows, head_count, HEAD)
    grad_blocks = grad_seq.reshape(block_count, block_rows, head_count, HEAD)
    key_heads = key_seq.reshape(length, head_count, HEAD)
    value_heads = value_seq.reshape(length, head_count, HEAD)

    def one_block(carry, block_items):
        key_grad, value_grad, offset_grad = carry
        block_number, bias_rows, query_rows, grad_rows, row_log = block_items
        scores = block_scores(query_rows, key_heads, bias_rows)
        probs = jnp.exp(scores - row_log[:, :, None])
        grad_weights = jnp.einsum(
            "ihd,jhd->hij", grad_rows, value_heads, preferred_element_type=jnp.float32
        )
        inner_sum = jnp.sum(probs * grad_weights, axis=-1, keepdims=True)
        grad_scores = (probs * (grad_weights - inner_sum)).astype(jnp.bfloat16)
        query_grad = (
            jnp.einsum("hij,jhd->ihd", grad_scores, key_heads, preferred_element_type=jnp.float32)
            * scale_factor
        )
        key_grad = (
            key_grad
            + jnp.einsum(
                "hij,ihd->jhd", grad_scores, query_rows, preferred_element_type=jnp.float32
            )
            * scale_factor
        )
        value_grad = value_grad + jnp.einsum(
            "hij,ihd->jhd",
            probs.astype(jnp.bfloat16),
            grad_rows,
            preferred_element_type=jnp.float32,
        )
        window_start = length - block_rows - block_number * block_rows
        current = lax.dynamic_slice_in_dim(offset_grad, window_start, window_width, 1)
        updated = current + bias_window_back(grad_scores, block_rows, length)
        offset_grad = lax.dynamic_update_slice_in_dim(offset_grad, updated, window_start, 1)
        return (
            (key_grad, value_grad, offset_grad),
            query_grad.astype(jnp.bfloat16).reshape(block_rows, local_width),
        )

    zero_heads = jnp.zeros((length, head_count, HEAD), jnp.float32)
    start_carry = (zero_heads, zero_heads, jnp.zeros((head_count, 2 * length - 1), jnp.float32))
    final_carry, query_grads = lax.scan(
        one_block,
        start_carry,
        (jnp.arange(block_count), bias_blocks, query_blocks, grad_blocks, log_totals),
    )
    key_grad, value_grad, offset_grad = final_carry
    return (
        query_grads.reshape(length, local_width),
        key_grad.astype(jnp.bfloat16).reshape(length, local_width),
        value_grad.astype(jnp.bfloat16).reshape(length, local_width),
        offset_grad,
    )


def shards(
    tokens,
    routes,
    buckets,
    gain_attn,
    w_query,
    w_key,
    w_value,
    w_out,
    bias_table,
    gain_ff,
    router,
    expert_up,
    expert_down,
    out_grad,
):
    seq_count, block_rows, model_width = tokens.shape
    seq_ways = lax.axis_size("seq")
    length = block_rows * seq_ways
    capacity = block_rows * 9 // 16
    expert_count = router.shape[1]
    slot_count = expert_count * capacity
    token_rows = seq_count * block_rows
    query_block = min(512, length)
    block_count = length // query_block
    full_query, full_key, full_value, full_out = (
        lax.all_gather(w_query, "fsdp", axis=0, tiled=True),
        lax.all_gather(w_key, "fsdp", axis=0, tiled=True),
        lax.all_gather(w_value, "fsdp", axis=0, tiled=True),
        lax.all_gather(w_out, "fsdp", axis=0, tiled=True),
    )
    inputs = tokens.astype(jnp.float32)
    first_scale = norm_scale(inputs)
    normed = (inputs * first_scale * gain_attn).astype(jnp.bfloat16)
    normed_rows = normed.reshape(token_rows, model_width)

    def project(weight):
        projected = jnp.dot(normed_rows, weight, preferred_element_type=jnp.float32)
        return projected.astype(jnp.bfloat16).reshape(seq_count, block_rows, model_width)

    query_heads, key_heads, value_heads = (
        lax.all_to_all(project(full_query), "seq", split_axis=2, concat_axis=1, tiled=True),
        lax.all_to_all(project(full_key), "seq", split_axis=2, concat_axis=1, tiled=True),
        lax.all_to_all(project(full_value), "seq", split_axis=2, concat_axis=1, tiled=True),
    )
    seq_place = lax.axis_index("seq")
    local_heads = model_width // seq_ways // HEAD
    table_here = lax.dynamic_slice_in_dim(bias_table, seq_place * local_heads, local_heads, 1)
    bucket_table = (buckets[:, None] == jnp.arange(bias_table.shape[0])[None, :]).astype(
        jnp.float32
    )
    offset_bias = jnp.dot(bucket_table, table_here, precision=PRECISE).T

    def bias_rows_of(block_number):
        return bias_window(offset_bias, block_number * query_block, query_block, length)

    bias_blocks = lax.map(bias_rows_of, jnp.arange(block_count))

    def forward_sequence(seq_items):
        return attend_forward(seq_items[0], seq_items[1], seq_items[2], bias_blocks, query_block)

    contexts, log_totals = lax.map(forward_sequence, (query_heads, key_heads, value_heads))
    context_tokens = lax.all_to_all(contexts, "seq", split_axis=1, concat_axis=2, tiled=True)
    context_rows = context_tokens.reshape(token_rows, model_width)
    attn_branch = jnp.dot(context_rows, full_out, preferred_element_type=jnp.float32)
    hidden = inputs + attn_branch.reshape(seq_count, block_rows, model_width)
    second_scale = norm_scale(hidden)
    ffnorm = hidden * second_scale * gain_ff
    ff_low = ffnorm.astype(jnp.bfloat16)
    logits = jnp.einsum("std,de->ste", ffnorm, router, precision=PRECISE)
    route_probs = jax.nn.softmax(logits, axis=-1)
    chosen = routes[:, :, 0]
    picked = (chosen[:, :, None] == jnp.arange(expert_count)[None, None, :]).astype(jnp.float32)
    gate_value = jnp.sum(route_probs * picked, axis=-1)
    earlier = jnp.cumsum(picked, axis=1) - picked
    slot_index = chosen * capacity + jnp.sum(earlier * picked, axis=-1).astype(jnp.int32)
    dispatch = (slot_index[:, None, :] == jnp.arange(slot_count)[None, :, None]).astype(
        jnp.bfloat16
    )
    dispatched = jnp.einsum("sct,std->scd", dispatch, ff_low, preferred_element_type=jnp.float32)
    dispatched = dispatched.astype(jnp.bfloat16).reshape(
        seq_count, expert_count, capacity, model_width
    )
    all_slots = lax.all_gather(dispatched, "seq", axis=0, tiled=True)
    whole_up, whole_down = (
        lax.all_gather(expert_up, "fsdp", axis=1, tiled=True),
        lax.all_gather(expert_down, "fsdp", axis=1, tiled=True),
    )
    pieces = (whole_up, whole_down)
    pre_piece = jnp.einsum(
        "secd,efd->secf", all_slots, pieces[0], preferred_element_type=jnp.float32
    )
    act_piece = gelu_slope(pre_piece)[0].astype(jnp.bfloat16)
    summed_out = jnp.einsum(
        "secf,efd->secd", act_piece, pieces[1], preferred_element_type=jnp.float32
    )
    pre_act = pre_piece
    expert_out = lax.psum_scatter(summed_out, "seq", scatter_dimension=0, tiled=True)
    token_expert = jnp.take_along_axis(
        expert_out.reshape(seq_count, slot_count, model_width), slot_index[:, :, None], axis=1
    )
    output = (hidden + gate_value[:, :, None] * token_expert).astype(jnp.bfloat16)
    upstream = out_grad.astype(jnp.float32)
    gate_grad = jnp.sum(upstream * token_expert, axis=-1)
    logit_grad = gate_value[:, :, None] * (picked - route_probs) * gate_grad[:, :, None]
    scaled_upstream = (gate_value[:, :, None] * upstream).astype(jnp.bfloat16)
    slot_grad = jnp.einsum(
        "sct,std->scd", dispatch, scaled_upstream, preferred_element_type=jnp.float32
    )
    slot_grad = slot_grad.astype(jnp.bfloat16).reshape(
        seq_count, expert_count, capacity, model_width
    )
    all_slot_grads = lax.all_gather(slot_grad, "seq", axis=0, tiled=True)
    pieces = (whole_up, whole_down)
    pre_piece = pre_act
    act_value, act_slope = gelu_slope(pre_piece)
    act_grad = jnp.einsum(
        "secd,efd->secf", all_slot_grads, pieces[1], preferred_element_type=jnp.float32
    )
    pre_grad = (act_grad * act_slope).astype(jnp.bfloat16)
    down_part = jnp.einsum(
        "secf,secd->efd",
        act_value.astype(jnp.bfloat16),
        all_slot_grads,
        preferred_element_type=jnp.float32,
    )
    up_part = jnp.einsum("secf,secd->efd", pre_grad, all_slots, preferred_element_type=jnp.float32)
    dispatch_grad = jnp.einsum(
        "secf,efd->secd", pre_grad, pieces[0], preferred_element_type=jnp.float32
    )
    dispatch_part = dispatch_grad
    dispatch_grad = lax.psum_scatter(dispatch_part, "seq", scatter_dimension=0, tiled=True)
    token_dispatch_grad = jnp.take_along_axis(
        dispatch_grad.reshape(seq_count, slot_count, model_width), slot_index[:, :, None], axis=1
    )
    ffnorm_grad = token_dispatch_grad + jnp.einsum(
        "ste,de->std", logit_grad, router, precision=PRECISE
    )
    router_grad = jnp.einsum("std,ste->de", ffnorm, logit_grad, precision=PRECISE)
    hidden_part, gain_ff_grad = norm_back(hidden, second_scale, gain_ff, ffnorm_grad)
    hidden_grad = upstream + hidden_part
    branch_grad = hidden_grad.astype(jnp.bfloat16).reshape(token_rows, model_width)
    out_weight_grad = jnp.einsum(
        "td,te->de", context_rows, branch_grad, preferred_element_type=jnp.float32
    )
    context_grad = jnp.einsum(
        "te,de->td", branch_grad, full_out, preferred_element_type=jnp.float32
    )
    context_grad = context_grad.astype(jnp.bfloat16).reshape(seq_count, block_rows, model_width)
    context_heads = lax.all_to_all(context_grad, "seq", split_axis=2, concat_axis=1, tiled=True)

    def backward_sequence(seq_items):
        return attend_backward(
            seq_items[0],
            seq_items[1],
            seq_items[2],
            seq_items[3],
            seq_items[4],
            bias_blocks,
            query_block,
        )

    query_grad, key_grad, value_grad, offset_grads = lax.map(
        backward_sequence, (query_heads, key_heads, value_heads, context_heads, log_totals)
    )
    query_back, key_back, value_back = (
        lax.all_to_all(query_grad, "seq", split_axis=1, concat_axis=2, tiled=True),
        lax.all_to_all(key_grad, "seq", split_axis=1, concat_axis=2, tiled=True),
        lax.all_to_all(value_grad, "seq", split_axis=1, concat_axis=2, tiled=True),
    )

    def weight_grad(grads):
        return jnp.einsum(
            "td,te->de",
            normed_rows,
            grads.reshape(token_rows, model_width),
            preferred_element_type=jnp.float32,
        )

    def input_grad(grads, weight):
        return jnp.einsum(
            "te,de->td",
            grads.reshape(token_rows, model_width),
            weight,
            preferred_element_type=jnp.float32,
        )

    normed_grad = (
        input_grad(query_back, full_query)
        + input_grad(key_back, full_key)
        + input_grad(value_back, full_value)
    )
    input_part, gain_attn_grad = norm_back(
        inputs, first_scale, gain_attn, normed_grad.reshape(seq_count, block_rows, model_width)
    )
    tokens_grad = hidden_grad + input_part
    table_part = jnp.dot(bucket_table.T, jnp.sum(offset_grads, axis=0).T, precision=PRECISE)
    table_full = lax.dynamic_update_slice_in_dim(
        jnp.zeros(bias_table.shape, jnp.float32), table_part, seq_place * local_heads, 1
    )
    gain_attn_sum, gain_ff_sum, router_sum, table_sum = lax.psum(
        (gain_attn_grad, gain_ff_grad, router_grad, table_full), ("seq", "fsdp")
    )
    query_weight_grad = weight_grad(query_back)
    key_weight_grad = weight_grad(key_back)
    value_weight_grad = weight_grad(value_back)
    shares = (
        lax.psum_scatter(query_weight_grad, "fsdp", scatter_dimension=0, tiled=True),
        lax.psum_scatter(key_weight_grad, "fsdp", scatter_dimension=0, tiled=True),
        lax.psum_scatter(value_weight_grad, "fsdp", scatter_dimension=0, tiled=True),
        lax.psum_scatter(out_weight_grad, "fsdp", scatter_dimension=0, tiled=True),
        lax.psum_scatter(up_part, "fsdp", scatter_dimension=1, tiled=True),
        lax.psum_scatter(down_part, "fsdp", scatter_dimension=1, tiled=True),
    )
    attn_sums = (
        lax.psum(shares[0].astype(jnp.bfloat16), "seq").astype(jnp.float32),
        lax.psum(shares[1].astype(jnp.bfloat16), "seq").astype(jnp.float32),
        lax.psum(shares[2].astype(jnp.bfloat16), "seq").astype(jnp.float32),
        lax.psum(shares[3].astype(jnp.bfloat16), "seq").astype(jnp.float32),
    )
    return (
        output,
        tokens_grad,
        gain_attn_sum,
        attn_sums[0],
        attn_sums[1],
        attn_sums[2],
        attn_sums[3],
        table_sum,
        gain_ff_sum,
        router_sum,
        shares[4],
        shares[5],
    )


def solution(mesh):
    in_specs = (
        P("fsdp", "seq", None),
        P("fsdp", "seq", None),
        P(),
        P(),
        P("fsdp", None),
        P("fsdp", None),
        P("fsdp", None),
        P("fsdp", None),
        P(),
        P(),
        P(),
        P(None, ("seq", "fsdp"), None),
        P(None, ("seq", "fsdp"), None),
        P("fsdp", "seq", None),
    )
    out_specs = (
        P("fsdp", "seq", None),
        P("fsdp", "seq", None),
        P(),
        P("fsdp", None),
        P("fsdp", None),
        P("fsdp", None),
        P("fsdp", None),
        P(),
        P(),
        P(),
        P(None, ("seq", "fsdp"), None),
        P(None, ("seq", "fsdp"), None),
    )
    return jax.shard_map(shards, mesh=mesh, in_specs=in_specs, out_specs=out_specs, check_vma=False)
```

profile of v0, /device:TPU:0, one launch (start us, length us, event | category | flops | bytes accessed | tf_op | source)
XLA Modules:
  0.0 1102.6 jit_solution(15459404114711115017)
XLA Ops:
  11.8 25.0 %all-gather.11.cloned.1.call-done = bf16[768,768]{1,0:T(8,128)(2,1)} async-done(((bf16[96,768]{1,0:T(8,128)(2,1)}), bf16[768,768]{1,0:T(8,128)(2,1)}) %all-gather.11.cloned.1.call-update) | async-done | bytes 1179664 | tf_op jit(solution)/shard_map/all_gather | solution.py:187
  39.8 3.1 reduce.17
  43.8 4.7 all-to-all-start.1
  48.5 14.2 %all-gather.13.cloned.1.call-done = bf16[768,768]{1,0:T(8,128)(2,1)} async-done(((bf16[96,768]{1,0:T(8,128)(2,1)}), bf16[768,768]{1,0:T(8,128)(2,1)}) %all-gather.13.cloned.1.call-update) | async-done | bytes 1179664 | tf_op jit(solution)/shard_map/all_gather | solution.py:188
  65.2 3.1 reduce.18
  69.1 4.6 all-to-all-start.2
  75.0 13.7 %all-gather.9.cloned.1.call-done = bf16[768,768]{1,0:T(8,128)(2,1)} async-done(((bf16[96,768]{1,0:T(8,128)(2,1)}), bf16[768,768]{1,0:T(8,128)(2,1)}) %all-gather.9.cloned.1.call-update) | async-done | bytes 1179664 | tf_op jit(solution)/shard_map/all_gather | solution.py:186
  91.1 3.1 reduce.16
  95.1 4.6 all-to-all-start
  99.7 137.8 %while.65 = (s32[]{:T(128)}, f32[2,3,512,1024]{3,2,1,0:T(8,128)}, s32[2]{0:T(128)S(1)}, f32[3,2047]{1,0:T(4,128)S(1)}, s32[]{:T(128)}, /*index=5*/s32[1]{0:T(128)}, s32[]{:T(128)}, s32[1]{0:T(128)}, f32[]{:T(128)}) while((s32[]{:T(128)}, f32[2,3,512,1024]{3,2,1,0:T(8,128)}, s32[2]{0:T(128)S(1)}, f32[3,2047]{1,0:T(4,128)S(1)}, s32[]{:T(128)}, ...), condition=%wide.region_1.2_spmd, body=%wide.region_0.0_spmd.sunk | while | flops 7 | bytes 97573008 | solution.py:216
  102.5 19.9 %copy.135 = f32[1,3,512,1536]{3,1,2,0:T(4,128)S(1)} copy(f32[1,3,512,1536]{3,2,1,0:T(8,128)S(1)} %broadcast_bitcast_fusion.2) | data formatting | bytes 18874368 | tf_op jit(solution)/shard_map/while
  122.4 5.8 slice.45
  128.2 13.2 %reshape.627 = f32[2357760]{0:T(1024)} reshape(f32[3,785920]{1,0:T(4,128)} %slice.45) | data formatting | bytes 18862080 | tf_op jit(solution)/shard_map/while
  141.4 15.6 %reshape.628 = f32[3,512,1535]{2,1,0:T(8,128)} reshape(f32[2357760]{0:T(1024)} %reshape.627) | data formatting | bytes 18862080 | tf_op jit(solution)/shard_map/while/body/eval_jaxpr/reshape | solution.py:46
  156.9 7.4 fusion.175
  166.8 19.9 %copy.135 = f32[1,3,512,1536]{3,1,2,0:T(4,128)S(1)} copy(f32[1,3,512,1536]{3,2,1,0:T(8,128)S(1)} %broadcast_bitcast_fusion.2) | data formatting | bytes 18874368 | tf_op jit(solution)/shard_map/while
  186.7 5.8 slice.45
  192.5 13.2 %reshape.627 = f32[2357760]{0:T(1024)} reshape(f32[3,785920]{1,0:T(4,128)} %slice.45) | data formatting | bytes 18862080 | tf_op jit(solution)/shard_map/while
  205.6 15.5 %reshape.628 = f32[3,512,1535]{2,1,0:T(8,128)} reshape(f32[2357760]{0:T(1024)} %reshape.627) | data formatting | bytes 18862080 | tf_op jit(solution)/shard_map/while/body/eval_jaxpr/reshape | solution.py:46
  221.2 7.3 fusion.175
  243.3 14.4 %while.66 = (s32[]{:T(128)}, bf16[2,512,192]{1,2,0:T(8,128)(2,1)S(1)}, f32[2,3,512]{2,1,0:T(4,128)S(1)}, bf16[2,512,3,64]{1,3,2,0:T(8,128)(2,1)S(1)}, bf16[1024,...) while((s32[]{:T(128)}, ...), condition=%wide.region_6.7_spmd, body=%wide.region_3.6_spmd.sunk | while | flops 415332864 | bytes 26795108 | solution.py:93
  243.3 3.9 fusion.178
  250.5 3.9 fusion.178
  258.2 4.3 reduce.19
  263.8 5.1 all-to-all-start.3
  269.4 11.1 %all-to-all-done.3 = bf16[4,2,24576]{2,1,0:T(2,128)(2,1)S(1)} async-done(((bf16[4,2,24576]{2,1,0:T(2,128)(2,1)}), bf16[4,2,24576]{2,1,0:T(2,128)(2,1)S(1)}, u32[]{:S(2)}, u32[]{:S(2)}) %all-to-all-start.3) | async-done | bytes 393248 | tf_op jit(solution)/shard_map/all_to_all | solution.py:222
  288.7 35.2 %all-gather.17.cloned.1.call-done = bf16[4,2,144,768]{3,2,0,1:T(8,128)(2,1)} async-done(((bf16[1,2,144,768]{3,2,0,1:T(8,128)(2,1)}), bf16[4,2,144,768]{3,2,0,1:T(8,128)(2,1)}) %all-gather.17.cloned.1.call-update) | async-done | bytes 1769488 | tf_op jit(solution)/shard_map/all_gather | solution.py:243
  324.0 6.2 fusion.42
  330.1 23.7 %all-gather.21.cloned.1.call-done = bf16[2,768,768]{2,1,0:T(8,128)(2,1)} async-done(((bf16[2,96,768]{2,1,0:T(8,128)(2,1)}), bf16[2,768,768]{2,1,0:T(8,128)(2,1)}) %all-gather.21.cloned.1.call-update) | async-done | bytes 2359312 | tf_op jit(solution)/shard_map/all_gather | solution.py:246
  353.8 5.5 fusion.51
  359.3 37.0 %all-gather.23.cloned.1.call-done = bf16[4,2,144,768]{3,2,0,1:T(8,128)(2,1)} async-done(((bf16[1,2,144,768]{3,2,0,1:T(8,128)(2,1)}), bf16[4,2,144,768]{3,2,0,1:T(8,128)(2,1)}) %all-gather.23.cloned.1.call-update) | async-done | bytes 1769488 | tf_op jit(solution)/shard_map/all_gather | solution.py:272
  396.3 5.6 fusion.38
  403.1 3.4 fusion.54
  407.8 246.5 %all-reduce.11.cloned.1.call-done = (f32[4,2,144,768]{3,2,0,1:T(8,128)}, f32[4,2,144,768]{3,2,0,1:T(8,128)}) async-done(((f32[4,2,144,768]{3,2,0,1:T(8,128)}, f32[4,2,144,768]{3,2,0,1:T(8,128)}), (f32[4,2,144,768]{3,2,0,1:T(8,128)}, f32[4,2,144,768]{3,2,0,1:T(8,128)})) %all-reduce.11.cloned.1.call-update) | async-done | bytes 7077904
  662.7 2.8 multiply_reduce_fusion.1
  667.0 3.1 reduce.20
  671.0 3.5 all-to-all-start.4
  676.5 9.9 all-to-all-done.4
  688.3 86.5 %while.67 = (s32[]{:T(128)}, f32[1024,3,64]{0,2,1:T(8,128)S(1)}, f32[1024,3,64]{0,2,1:T(8,128)}, f32[3,2047]{1,0:T(4,128)S(1)}, bf16[2,512,192]{1,2,0:T(8,128)(2...) while((s32[]{:T(128)}, f32[1024,3,64]{0,2,1:T(8,128)S(1)}, ...), condition=%wide.region_21.23_spmd.clone, body=%wide.region_18.22_spmd.clone.sunk | while | flops 1026685440 | bytes 112782616 | solution.py:146
  691.8 4.4 multiply_reduce_fusion.5
  700.2 4.1 pad.32
  704.3 10.4 reshape.629
  714.7 7.7 reshape.630
  722.4 5.7 pad_convert_fusion.2
  734.3 4.3 multiply_reduce_fusion.5
  739.2 2.7 fusion.192
  743.8 4.1 pad.32
  747.9 10.4 reshape.629
  758.3 7.5 reshape.630
  765.8 5.7 pad_convert_fusion.2
  771.5 2.5 bitcast_reduce_fusion.2
  778.0 4.9 reduce.23
  783.5 13.5 %all_to_all.120 = bf16[4,2,24576]{2,1,0:T(2,128)(2,1)S(1)} all-to-all(bf16[4,2,24576]{2,1,0:T(2,128)(2,1)S(1)} %reshape.621), channel_id=1, replica_groups=mesh['seq'=4,'fsdp'=8] {'seq'}, dimensions={0} | all-to-all | bytes 786432 | tf_op jit(solution)/shard_map/all_to_all | solution.py:328
  804.7 4.2 reduce.22
  809.5 13.7 %all_to_all.121 = bf16[4,2,24576]{2,1,0:T(2,128)(2,1)S(1)} all-to-all(bf16[4,2,24576]{2,1,0:T(2,128)(2,1)S(1)} %reshape.619), channel_id=1, replica_groups=mesh['seq'=4,'fsdp'=8] {'seq'}, dimensions={0} | all-to-all | bytes 786432 | tf_op jit(solution)/shard_map/all_to_all | solution.py:327
  827.8 4.2 reduce.21
  832.6 13.8 %all_to_all.122 = bf16[4,2,24576]{2,1,0:T(2,128)(2,1)S(1)} all-to-all(bf16[4,2,24576]{2,1,0:T(2,128)(2,1)S(1)} %reshape.617), channel_id=1, replica_groups=mesh['seq'=4,'fsdp'=8] {'seq'}, dimensions={0} | all-to-all | bytes 786432 | tf_op jit(solution)/shard_map/all_to_all | solution.py:326
  853.5 37.8 %reduce-scatter.11.cloned.1.call-done = f32[96,768]{1,0:T(8,128)} async-done(((f32[768,768]{1,0:T(8,128)}), f32[96,768]{1,0:T(8,128)}) %reduce-scatter.11.cloned.1.call-update) | async-done | bytes 294928 | tf_op jit(solution)/shard_map/reduce_scatter | solution.py:368
  892.9 44.6 %reduce-scatter.9.cloned.1.call-done = f32[96,768]{1,0:T(8,128)} async-done(((f32[768,768]{1,0:T(8,128)}), f32[96,768]{1,0:T(8,128)}) %reduce-scatter.9.cloned.1.call-update) | async-done | bytes 294928 | tf_op jit(solution)/shard_map/reduce_scatter | solution.py:367
  939.2 6.2 convolution_bitcast_fusion
  945.5 6.3 convolution_bitcast_fusion.1
  960.2 40.3 %all-reduce.5 = (f32[768]{0:T(1024)}, f32[32,12]{0,1:T(8,128)}, f32[768]{0:T(1024)}, f32[768,2]{0,1:T(2,128)}) all-reduce(f32[768]{0:T(1024)S(1)} %get-tuple-element.436, f32[32,12]{0,1:T(8,128)S(1)} %dynamic_update_slice.45, f32[768]{0:T(1024)S(1)} %copy-done.37, ...), channel_id=1, replica_groups=mesh['seq'=4,'fsdp'=8] {'seq','fsdp'}, use_global_device_ids=true, to_apply=%region_24.26 | all-reduce | flops 3456 | bytes 27648 | tf_op jit(solution)/shard_map/psum | solution.py:360
  1008.3 29.3 %reduce-scatter.19.cloned.1.call-done = f32[2,96,768]{2,1,0:T(8,128)} async-done(((f32[2,768,768]{2,1,0:T(8,128)}), f32[2,96,768]{2,1,0:T(8,128)}) %reduce-scatter.19.cloned.1.call-update) | async-done | bytes 589840 | tf_op jit(solution)/shard_map/reduce_scatter | solution.py:372
  1037.6 58.2 %reduce-scatter.17.cloned.1.call-done = f32[2,96,768]{2,1,0:T(8,128)} async-done(((f32[2,768,768]{2,1,0:T(8,128)}), f32[2,96,768]{2,1,0:T(8,128)}) %reduce-scatter.17.cloned.1.call-update) | async-done | bytes 589840 | tf_op jit(solution)/shard_map/reduce_scatter | solution.py:371
  (292 shorter events, 118.1 us)
Async XLA Ops:
  7.2 67.1 %copy-start = (f32[32,12]{0,1:T(8,128)S(1)}, f32[32,12]{0,1:T(8,128)}, u32[]{:S(2)}) copy-start(f32[32,12]{0,1:T(8,128)} %param.30) | copy-start | bytes 4612
  7.2 55.5 %copy-start.6 = (bf16[1,256,768]{2,1,0:T(8,128)(2,1)S(1)}, bf16[1,256,768]{2,1,0:T(8,128)(2,1)}, u32[]{:S(2)}) copy-start(bf16[1,256,768]{2,1,0:T(8,128)(2,1)} %param.22) | copy-start | bytes 1179652
  7.2 55.5 %copy-start.24 = (f32[768]{0:T(1024)S(1)}, f32[768]{0:T(1024)}, u32[]{:S(2)}) copy-start(f32[768]{0:T(1024)} %param.25) | copy-start | bytes 9220
  7.2 29.5 %all-gather.11.cloned.1.call-start = ((), (), s32[]{:S(2)}) async-start(), calls=%async_computation.15 | async-start | bytes 1327104 | tf_op jit(solution)/shard_map/all_gather | solution.py:187
  8.0 54.8 %all-gather.13.cloned.1.call-start = ((), (), s32[]{:S(2)}) async-start(), calls=%async_computation.16 | async-start | bytes 1327104 | tf_op jit(solution)/shard_map/all_gather | solution.py:188
  8.7 80.0 %all-gather.9.cloned.1.call-start = ((), (), s32[]{:S(2)}) async-start(), calls=%async_computation.14 | async-start | bytes 1327104 | tf_op jit(solution)/shard_map/all_gather | solution.py:186
  9.4 272.8 %all-gather.15.cloned.1.call-start = ((), (), s32[]{:S(2)}) async-start(), calls=%async_computation.17 | async-start | bytes 1327104 | tf_op jit(solution)/shard_map/all_gather | solution.py:189
  11.8 76.9 %copy-start.30 = (f32[256]{0:T(256)}, f32[256]{0:T(256)S(1)}, u32[]{:S(2)}) copy-start(f32[256]{0:T(256)S(1)} %get-tuple-element.505) | copy-start | bytes 3076
  43.8 30.6 %copy-start.42 = (s32[2047]{0:T(1024)S(1)}, s32[2047]{0:T(1024)}, u32[]{:S(2)}) copy-start(s32[2047]{0:T(1024)} %param.24) | copy-start | bytes 24568
  43.8 25.4 %all-to-all-start.1 = ((bf16[4,2,24576]{2,1,0:T(2,128)(2,1)}), bf16[4,2,24576]{2,1,0:T(2,128)(2,1)S(1)}, u32[]{:S(2)}, u32[]{:S(2)}) async-start(bf16[4,2,24576]{2,1,0:T(2,128)(2,1)} %reshape.609), calls=%async_computation.1 | async-start | bytes 786432 | tf_op jit(solution)/shard_map/all_to_all | solution.py:202
  69.1 26.0 %copy-start.18 = (bf16[4,2,24576]{2,1,0:T(2,128)(2,1)}, bf16[4,2,24576]{2,1,0:T(2,128)(2,1)S(1)}, u32[]{:S(2)}) copy-start(bf16[4,2,24576]{2,1,0:T(2,128)(2,1)S(1)} %all-to-all-done.1) | copy-start | bytes 1179652
  69.1 26.0 %all-to-all-start.2 = ((bf16[4,2,24576]{2,1,0:T(2,128)(2,1)}), bf16[4,2,24576]{2,1,0:T(2,128)(2,1)S(1)}, u32[]{:S(2)}, u32[]{:S(2)}) async-start(bf16[4,2,24576]{2,1,0:T(2,128)(2,1)} %reshape.611), calls=%async_computation.2 | async-start | bytes 786432 | tf_op jit(solution)/shard_map/all_to_all | solution.py:203
  73.7 215.0 %all-gather.19.cloned.1.call-start = ((), (), s32[]{:S(2)}) async-start(), calls=%async_computation.19 | async-start | bytes 2654208 | tf_op jit(solution)/shard_map/all_gather | solution.py:245
  95.1 4.6 copy-start.20
  95.1 145.3 %all-to-all-start = ((bf16[4,2,24576]{2,1,0:T(2,128)(2,1)}), bf16[4,2,24576]{2,1,0:T(2,128)(2,1)}, u32[]{:S(2)}, u32[]{:S(2)}) async-start(bf16[4,2,24576]{2,1,0:T(2,128)(2,1)} %reshape.607), calls=%async_computation | async-start | bytes 786432 | tf_op jit(solution)/shard_map/all_to_all | solution.py:201
  99.7 137.9 %copy-start.26 = (s32[1,256,1]{1,2,0:T(1,128)S(1)}, s32[1,256,1]{1,2,0:T(1,128)}, u32[]{:S(2)}) copy-start(s32[1,256,1]{1,2,0:T(1,128)} %param.23) | copy-start | bytes 3076
  99.7 138.5 %copy-start.19 = (bf16[4,2,24576]{2,1,0:T(2,128)(2,1)S(1)}, bf16[4,2,24576]{2,1,0:T(2,128)(2,1)}, u32[]{:S(2)}) copy-start(bf16[4,2,24576]{2,1,0:T(2,128)(2,1)} %copy-done.18) | copy-start | bytes 1179652
  237.5 1.8 copy-start.21
  257.7 23.6 %copy-start.4 = (bf16[2,512,3,64]{1,3,2,0:T(8,128)(2,1)}, bf16[2,512,3,64]{1,3,2,0:T(8,128)(2,1)S(1)}, u32[]{:S(2)}) copy-start(bf16[2,512,3,64]{1,3,2,0:T(8,128)(2,1)S(1)} %get-tuple-element.797) | copy-start | bytes 1179652
  257.7 23.6 %copy-start.9 = (bf16[1024,3,64]{0,2,1:T(8,128)(2,1)}, bf16[1024,3,64]{0,2,1:T(8,128)(2,1)S(1)}, u32[]{:S(2)}) copy-start(bf16[1024,3,64]{0,2,1:T(8,128)(2,1)S(1)} %get-tuple-element.798) | copy-start | bytes 1179652
  258.2 24.1 %copy-start.7 = (bf16[1,256,768]{2,1,0:T(8,128)(2,1)S(1)}, bf16[1,256,768]{2,1,0:T(8,128)(2,1)}, u32[]{:S(2)}) copy-start(bf16[1,256,768]{2,1,0:T(8,128)(2,1)} %param.22) | copy-start | bytes 1179652
  263.8 16.7 %all-to-all-start.3 = ((bf16[4,2,24576]{2,1,0:T(2,128)(2,1)}), bf16[4,2,24576]{2,1,0:T(2,128)(2,1)S(1)}, u32[]{:S(2)}, u32[]{:S(2)}) async-start(bf16[4,2,24576]{2,1,0:T(2,128)(2,1)} %reshape.613), calls=%async_computation.3 | async-start | bytes 786432 | tf_op jit(solution)/shard_map/all_to_all | solution.py:222
  268.9 55.0 %all-gather.17.cloned.1.call-start = ((), (), s32[]{:S(2)}) async-start(), calls=%async_computation.18 | async-start | bytes 2211840 | tf_op jit(solution)/shard_map/all_gather | solution.py:243
  269.4 14.8 %copy-start.22 = (f32[768]{0:T(1024)S(1)}, f32[768]{0:T(1024)}, u32[]{:S(2)}) copy-start(f32[768]{0:T(1024)} %param.31) | copy-start | bytes 9220
  281.3 4.9 copy-start.34
  281.9 5.2 copy-start.13
  284.2 381.4 %copy-start.2 = (f32[1,256,768]{2,1,0:T(8,128)}, f32[1,256,768]{2,1,0:T(8,128)S(1)}, u32[]{:S(2)}) copy-start(f32[1,256,768]{2,1,0:T(8,128)S(1)} %get-tuple-element.509) | copy-start | bytes 2359300
  284.2 381.4 %copy-start.28 = (f32[256]{0:T(256)}, f32[256]{0:T(256)S(1)}, u32[]{:S(2)}) copy-start(f32[256]{0:T(256)S(1)} %get-tuple-element.507) | copy-start | bytes 3076
  285.4 68.4 %all-gather.21.cloned.1.call-start = ((), (), s32[]{:S(2)}) async-start(), calls=%async_computation.20 | async-start | bytes 2654208 | tf_op jit(solution)/shard_map/all_gather | solution.py:246
  286.1 110.2 %all-gather.23.cloned.1.call-start = ((), (), s32[]{:S(2)}) async-start(), calls=%async_computation.21 | async-start | bytes 2211840 | tf_op jit(solution)/shard_map/all_gather | solution.py:272
  287.1 375.6 %copy-start.32 = (f32[256]{0:T(256)}, f32[256]{0:T(256)S(1)}, u32[]{:S(2)}) copy-start(f32[256]{0:T(256)S(1)} %get-tuple-element.496) | copy-start | bytes 3076
  287.1 375.6 %copy-start.35 = (f32[256,2]{0,1:T(2,128)}, f32[256,2]{0,1:T(2,128)S(1)}, u32[]{:S(2)}) copy-start(f32[256,2]{0,1:T(2,128)S(1)} %get-tuple-element.497) | copy-start | bytes 6148
  288.3 366.0 %all-reduce.11.cloned.1.call-start = ((), (), s32[]{:S(2)}) async-start(), calls=%async_computation.28 | async-start | bytes 14155776
  396.3 6.8 copy-start.41
  401.9 1.2 copy-start.45
  658.4 2.0 copy-start.14
  660.4 5.4 copy-start.12
  662.7 3.7 copy-start.38
  665.8 10.6 copy-start.10
  671.0 15.4 %all-to-all-start.4 = ((bf16[4,2,24576]{2,1,0:T(2,128)(2,1)}), bf16[4,2,24576]{2,1,0:T(2,128)(2,1)S(1)}, u32[]{:S(2)}, u32[]{:S(2)}) async-start(bf16[4,2,24576]{2,1,0:T(2,128)(2,1)} %reshape.615), calls=%async_computation.4 | async-start | bytes 786432 | tf_op jit(solution)/shard_map/all_to_all | solution.py:309
  674.4 175.8 %reduce-scatter.15.cloned.1.call-start = ((), (), s32[]{:S(2)}) async-start(), calls=%async_computation.25 | async-start | bytes 2654208 | tf_op jit(solution)/shard_map/reduce_scatter | solution.py:370
  676.4 11.8 %copy-start.5 = (bf16[2,512,3,64]{1,3,2,0:T(8,128)(2,1)S(1)}, bf16[2,512,3,64]{1,3,2,0:T(8,128)(2,1)}, u32[]{:S(2)}) copy-start(bf16[2,512,3,64]{1,3,2,0:T(8,128)(2,1)} %copy-done.4) | copy-start | bytes 1179652
  676.5 175.4 %reduce-scatter.13.cloned.1.call-start = ((), (), s32[]{:S(2)}) async-start(), calls=%async_computation.24 | async-start | bytes 2654208 | tf_op jit(solution)/shard_map/reduce_scatter | solution.py:369
  699.5 4.8 copy-start.16
  743.1 4.8 copy-start.16
  778.0 23.6 %copy-start.8 = (bf16[1,256,768]{2,1,0:T(8,128)(2,1)S(1)}, bf16[1,256,768]{2,1,0:T(8,128)(2,1)}, u32[]{:S(2)}) copy-start(bf16[1,256,768]{2,1,0:T(8,128)(2,1)} %param.22) | copy-start | bytes 1179652
  778.0 23.6 %copy-start.25 = (f32[768]{0:T(1024)S(1)}, f32[768]{0:T(1024)}, u32[]{:S(2)}) copy-start(f32[768]{0:T(1024)} %param.25) | copy-start | bytes 9220
  778.0 23.6 %copy-start.31 = (f32[256]{0:T(256)S(1)}, f32[256]{0:T(256)}, u32[]{:S(2)}) copy-start(f32[256]{0:T(256)} %copy-done.30) | copy-start | bytes 3076
  803.8 87.5 %reduce-scatter.11.cloned.1.call-start = ((), (), s32[]{:S(2)}) async-start(), calls=%async_computation.23 | async-start | bytes 2654208 | tf_op jit(solution)/shard_map/reduce_scatter | solution.py:368
  824.7 2.5 copy-start.17
  827.1 110.4 %reduce-scatter.9.cloned.1.call-start = ((), (), s32[]{:S(2)}) async-start(), calls=%async_computation.22 | async-start | bytes 2654208 | tf_op jit(solution)/shard_map/reduce_scatter | solution.py:367
  850.1 151.6 %all-reduce.13.cloned.1.call-start = ((), (), s32[]{:S(2)}) async-start(), calls=%async_computation.29 | async-start | bytes 1179648 | tf_op jit(solution)/shard_map/psum | solution.py:375
  939.1 98.5 %reduce-scatter.19.cloned.1.call-start = ((), (), s32[]{:S(2)}) async-start(), calls=%async_computation.27 | async-start | bytes 5308416 | tf_op jit(solution)/shard_map/reduce_scatter | solution.py:372
  945.4 150.4 %reduce-scatter.17.cloned.1.call-start = ((), (), s32[]{:S(2)}) async-start(), calls=%async_computation.26 | async-start | bytes 5308416 | tf_op jit(solution)/shard_map/reduce_scatter | solution.py:371
  951.7 1.1 copy-start.3
  951.7 1.1 copy-start.23
  951.7 1.1 copy-start.27
  951.7 1.1 copy-start.29
  951.7 1.1 copy-start.33
  951.8 1.7 copy-start.43
  956.3 3.9 copy-start.37
  956.3 44.2 %copy-start.11 = (f32[1,256,768]{2,1,0:T(8,128)S(1)}, f32[1,256,768]{2,1,0:T(8,128)}, u32[]{:S(2)}) copy-start(f32[1,256,768]{2,1,0:T(8,128)} %copy-done.10) | copy-start | bytes 2359300
  956.3 44.2 %copy-start.40 = (f32[256]{0:T(256)S(1)}, f32[256]{0:T(256)}, u32[]{:S(2)}) copy-start(f32[256]{0:T(256)} %get-tuple-element.504) | copy-start | bytes 3076
  956.3 139.5 %copy-start.1 = (f32[32,12]{0,1:T(8,128)S(1)}, f32[32,12]{0,1:T(8,128)}, u32[]{:S(2)}) copy-start(f32[32,12]{0,1:T(8,128)} %param.30) | copy-start | bytes 4612
  (5 other events, 5.1 us)
Sparse Core Ops, SparseCore 0:
  9.9 26.7 all-gather.10
  38.6 24.0 all-gather.12
  64.6 24.0 all-gather.8
  90.4 24.0 all-gather.14
  116.3 29.0 all-gather.18
  285.5 38.4 all-gather.16
  325.9 27.8 all-gather.20
  355.9 40.3 all-gather.22
  406.6 247.5 all-reduce.10
  678.3 43.8 reduce-scatter.14
  803.9 41.5 reduce-scatter.12
  848.7 42.5 reduce-scatter.10
  895.0 42.4 reduce-scatter.8
  940.5 39.9 all-reduce.12
  984.4 53.1 reduce-scatter.18
  1041.9 53.8 reduce-scatter.16
where the time goes:
time: 1110 us; the launch traced here: 1100 us
  waiting for transfers between devices  590 us (53%)
  local copies, waits for them, and re-layouts  214 us (19%)
  matrix products  94.6 us (9%)
  blocking collectives  81.3 us (7%)
  other arithmetic  71.7 us (6%)
  starting transfers between devices  23.5 us (2%)
  between operations  15.2 us (1%)
  loops' own time  12.8 us (1%)
    unnamed x17, waiting for transfers between devices  250 us
    while x16, local copies, waits for them, and re-layouts  89.2 us
    reduce_scatter x1, waiting for transfers between devices, shards(): lax.psum_scatter(up_part, 'fsdp', scatter_dimension=1, tiled=True)  58.2 us
    reduce_scatter x1, waiting for transfers between devices, shards(): lax.psum_scatter(query_weight_grad, 'fsdp', scatter_dimension=0, tiled=True)  44.6 us
    psum x1, blocking collectives, shards(): lax.psum((gain_attn_grad, gain_ff_grad, router_grad, table_full), ('seq',...  40.3 us
    reduce_scatter x1, waiting for transfers between devices, shards(): lax.psum_scatter(key_weight_grad, 'fsdp', scatter_dimension=0, tiled=True)  37.8 us
    all_gather x1, waiting for transfers between devices, shards(): all_slot_grads = lax.all_gather(slot_grad, 'seq', axis=0, tiled=True)  37 us
    all_gather x1, waiting for transfers between devices, shards(): all_slots = lax.all_gather(dispatched, 'seq', axis=0, tiled=True)  35.2 us
  transfers between devices with their start and end apart: 21, of which 13 were waited for; matrix products, arithmetic and copies ran while one was open for 32% of the time, Pallas kernels for 0%

commit v1 on v0

v1 whole, which is shorter than its diff:
```python
import jax
import jax.numpy as jnp
from jax import lax
from jax.experimental import pallas as pl
from jax.experimental.pallas import tpu as pltpu
from jax.sharding import PartitionSpec as P

HEAD = 64
EPSILON = 1e-06
PRECISE = lax.Precision.HIGHEST
ROOT_HALF = 0.7071067811865476
DENSITY = 0.3989422804014327
LOG2E = 1.4426950408889634
SCORE_SCALE = HEAD ** (-0.5)
VMEM_LIMIT = 56 * 1024 * 1024
BF16 = jnp.bfloat16
F32 = jnp.float32


def dot_of(left, right, left_dim, right_dim):
    return lax.dot_general(
        left, right, (((left_dim,), (right_dim,)), ((), ())), preferred_element_type=F32
    )


def norm_scale(values):
    return lax.rsqrt(jnp.mean(values * values, axis=-1, keepdims=True) + EPSILON)


def bias_tiles_kernel(reversed_ref, tiles_ref):
    rows = tiles_ref.shape[1]
    width = reversed_ref.shape[2]
    for head in range(tiles_ref.shape[0]):
        line = jnp.broadcast_to(reversed_ref[head], (rows, width))
        skewed = pltpu.roll(line, width - (rows - 1), 1, stride=1, stride_axis=0)
        tiles_ref[head] = skewed[:, : tiles_ref.shape[2]]


def bias_tiles(reversed_bias, rows, columns):
    heads = reversed_bias.shape[0]
    return pl.pallas_call(
        bias_tiles_kernel,
        out_shape=jax.ShapeDtypeStruct((heads, rows, columns), F32),
        in_specs=[pl.BlockSpec(memory_space=pltpu.VMEM)],
        out_specs=pl.BlockSpec(memory_space=pltpu.VMEM),
        compiler_params=pltpu.CompilerParams(vmem_limit_bytes=VMEM_LIMIT),
        name="bias_tiles",
    )(reversed_bias)


def tile_start(me, key_block, query_block, ways, rows):
    key_place = lax.rem(me + key_block, ways)
    query_place = lax.rem(me + query_block, ways)
    return pl.multiple_of((query_place - key_place + ways - 1) * rows, rows)


def attend_kernel(me_ref, qkv_ref, tiles_ref, context_ref, total_ref, context_t):
    heads, rows = tiles_ref.shape[0], tiles_ref.shape[1]
    length = qkv_ref.shape[1]
    ways = length // rows
    width = heads * HEAD
    me = me_ref[0]
    for head in range(heads):
        lanes = slice(head * HEAD, (head + 1) * HEAD)
        key_lanes = slice(width + head * HEAD, width + (head + 1) * HEAD)
        value_lanes = slice(2 * width + head * HEAD, 2 * width + (head + 1) * HEAD)

        def one_block(query_block, _):
            query_rows = pl.ds(pl.multiple_of(query_block * rows, rows), rows)
            query = qkv_ref[0, query_rows, lanes]
            scores = []
            for key_block in range(ways):
                key = qkv_ref[0, key_block * rows : (key_block + 1) * rows, key_lanes]
                start = tile_start(me, key_block, query_block, ways, rows)
                scores.append(
                    dot_of(key, query, 1, 1) * (SCORE_SCALE * LOG2E)
                    + tiles_ref[head, :, pl.ds(start, rows)]
                )
            top = scores[0]
            for tile in scores[1:]:
                top = jnp.maximum(top, tile)
            top = jnp.max(top, axis=0, keepdims=True)
            total = jnp.zeros((1, rows), F32)
            context = jnp.zeros((HEAD, rows), F32)
            for key_block in range(ways):
                value = qkv_ref[0, key_block * rows : (key_block + 1) * rows, value_lanes]
                shifted = jnp.exp2(scores[key_block] - top)
                total = total + jnp.sum(shifted, axis=0, keepdims=True)
                context = context + dot_of(value, shifted.astype(BF16), 0, 0)
            context_t[lanes, query_rows] = context / total
            total_ref[0, head, :, query_rows] = top + jnp.log2(total)
            return 0

        lax.fori_loop(0, ways, one_block, 0)
    context_ref[0] = context_t[...].T.astype(BF16)


def attend(me, qkv, tiles):
    seq_count, length, triple = qkv.shape
    heads, rows, columns = tiles.shape
    width = triple // 3
    return pl.pallas_call(
        attend_kernel,
        grid=(seq_count,),
        out_shape=(
            jax.ShapeDtypeStruct((seq_count, length, width), BF16),
            jax.ShapeDtypeStruct((seq_count, heads, 1, length), F32),
        ),
        in_specs=[
            pl.BlockSpec(memory_space=pltpu.SMEM),
            pl.BlockSpec((1, length, triple), lambda i: (i, 0, 0)),
            pl.BlockSpec((heads, rows, columns), lambda i: (0, 0, 0)),
        ],
        out_specs=(
            pl.BlockSpec((1, length, width), lambda i: (i, 0, 0)),
            pl.BlockSpec((1, heads, 1, length), lambda i: (i, 0, 0, 0)),
        ),
        scratch_shapes=[pltpu.VMEM((width, length), F32)],
        compiler_params=pltpu.CompilerParams(vmem_limit_bytes=VMEM_LIMIT),
        name="attend",
    )(me, qkv, tiles)


def attend_back_kernel(
    me_ref, qkv_ref, grad_ref, total_ref, tiles_ref, out_ref, offset_ref,
    query_t, key_sum, value_sum, tile_sum,
):
    heads, rows = tiles_ref.shape[0], tiles_ref.shape[1]
    length = qkv_ref.shape[1]
    ways = length // rows
    width = heads * HEAD
    me = me_ref[0]
    key_sum[...] = jnp.zeros(key_sum.shape, F32)
    value_sum[...] = jnp.zeros(value_sum.shape, F32)
    for head in range(heads):
        lanes = slice(head * HEAD, (head + 1) * HEAD)
        key_lanes = slice(width + head * HEAD, width + (head + 1) * HEAD)
        value_lanes = slice(2 * width + head * HEAD, 2 * width + (head + 1) * HEAD)
        tile_sum[...] = jnp.zeros(tile_sum.shape, F32)

        def one_block(query_block, _):
            query_rows = pl.ds(pl.multiple_of(query_block * rows, rows), rows)
            query = qkv_ref[0, query_rows, lanes]
            grad = grad_ref[0, query_rows, lanes]
            total = total_ref[0, head, :, query_rows]
            probs, weight_grads = [], []
            inner = jnp.zeros((1, rows), F32)
            for key_block in range(ways):
                key_rows = slice(key_block * rows, (key_block + 1) * rows)
                start = tile_start(me, key_block, query_block, ways, rows)
                scores = (
                    dot_of(qkv_ref[0, key_rows, key_lanes], query, 1, 1)
                    * (SCORE_SCALE * LOG2E)
                    + tiles_ref[head, :, pl.ds(start, rows)]
                )
                prob = jnp.exp2(scores - total)
                weight_grad = dot_of(qkv_ref[0, key_rows, value_lanes], grad, 1, 1)
                inner = inner + jnp.sum(prob * weight_grad, axis=0, keepdims=True)
                value_sum[key_rows, lanes] += dot_of(prob.astype(BF16), grad, 1, 0)
                probs.append(prob)
                weight_grads.append(weight_grad)
            query_grad = jnp.zeros((HEAD, rows), F32)
            for key_block in range(ways):
                key_rows = slice(key_block * rows, (key_block + 1) * rows)
                start = tile_start(me, key_block, query_block, ways, rows)
                score_grad = probs[key_block] * (weight_grads[key_block] - inner)
                tile_sum[:, pl.ds(start, rows)] += score_grad
                score_low = score_grad.astype(BF16)
                key_sum[key_rows, lanes] += dot_of(score_low, query, 1, 0)
                query_grad = query_grad + dot_of(
                    qkv_ref[0, key_rows, key_lanes], score_low, 0, 0
                )
            query_t[lanes, query_rows] = query_grad
            return 0

        lax.fori_loop(0, ways, one_block, 0)
        folded, half = tile_sum[...], rows // 2
        while half:
            folded = pltpu.roll(folded[:half], half, 1) + folded[half:]
            half //= 2
        offset_ref[0, head] = folded
    out_ref[0, :, :width] = (query_t[...].T * SCORE_SCALE).astype(BF16)
    out_ref[0, :, width : 2 * width] = (key_sum[...] * SCORE_SCALE).astype(BF16)
    out_ref[0, :, 2 * width :] = value_sum[...].astype(BF16)


def attend_back(me, qkv, grads, totals, tiles, span):
    seq_count, length, triple = qkv.shape
    heads, rows, columns = tiles.shape
    width = triple // 3
    return pl.pallas_call(
        attend_back_kernel,
        grid=(seq_count,),
        out_shape=(
            jax.ShapeDtypeStruct((seq_count, length, triple), BF16),
            jax.ShapeDtypeStruct((seq_count, heads, 1, span), F32),
        ),
        in_specs=[
            pl.BlockSpec(memory_space=pltpu.SMEM),
            pl.BlockSpec((1, length, triple), lambda i: (i, 0, 0)),
            pl.BlockSpec((1, length, width), lambda i: (i, 0, 0)),
            pl.BlockSpec((1, heads, 1, length), lambda i: (i, 0, 0, 0)),
            pl.BlockSpec((heads, rows, columns), lambda i: (0, 0, 0)),
        ],
        out_specs=(
            pl.BlockSpec((1, length, triple), lambda i: (i, 0, 0)),
            pl.BlockSpec((1, heads, 1, span), lambda i: (i, 0, 0, 0)),
        ),
        scratch_shapes=[
            pltpu.VMEM((width, length), F32),
            pltpu.VMEM((length, width), F32),
            pltpu.VMEM((length, width), F32),
            pltpu.VMEM((rows, span), F32),
        ],
        compiler_params=pltpu.CompilerParams(vmem_limit_bytes=VMEM_LIMIT),
        name="attend_back",
    )(me, qkv, grads, totals, tiles)


def experts_kernel(slots_ref, grads_ref, weights_ref, out_ref, slot_grad_ref, weight_grad_ref):
    units = weights_ref.shape[0] * weights_ref.shape[4]
    model_width = weights_ref.shape[5]
    up = weights_ref[:, 0, 0, 0].reshape(units, model_width)
    down = weights_ref[:, 0, 1, 0].reshape(units, model_width)
    slots = slots_ref[0]
    grads = grads_ref[0]
    pre = dot_of(slots, up, 1, 1)
    normal_cdf = 0.5 * (1.0 + lax.erf(pre * ROOT_HALF))
    act = (pre * normal_cdf).astype(BF16)
    slope = normal_cdf + pre * jnp.exp(-0.5 * pre * pre) * DENSITY
    act_grad = dot_of(grads, down, 1, 1)
    pre_grad = (act_grad * slope).astype(BF16)
    returned = dot_of(act, down, 1, 0)
    back = dot_of(pre_grad, up, 1, 0)
    first = pl.program_id(1) == 0

    @pl.when(first)
    def _():
        out_ref[0] = returned
        slot_grad_ref[0] = back

    @pl.when(jnp.logical_not(first))
    def _():
        out_ref[0] += returned
        slot_grad_ref[0] += back

    part_shape = weight_grad_ref.shape[0:1] + weight_grad_ref.shape[4:]
    weight_grad_ref[:, 0, 0, 0] = dot_of(pre_grad, slots, 0, 0).astype(BF16).reshape(part_shape)
    weight_grad_ref[:, 0, 1, 0] = dot_of(act, grads, 0, 0).astype(BF16).reshape(part_shape)


def experts(slots, grads, weights):
    expert_count, rows, model_width = slots.shape
    shards, groups, kinds, _, units, _ = weights.shape
    row_spec = pl.BlockSpec((1, rows, model_width), lambda e, j: (e, 0, 0))
    weight_spec = pl.BlockSpec(
        (shards, 1, kinds, 1, units, model_width), lambda e, j: (0, j, 0, e, 0, 0)
    )
    flops = 12 * expert_count * rows * model_width * shards * groups * units
    return pl.pallas_call(
        experts_kernel,
        grid=(expert_count, groups),
        out_shape=(
            jax.ShapeDtypeStruct(slots.shape, F32),
            jax.ShapeDtypeStruct(slots.shape, F32),
            jax.ShapeDtypeStruct(weights.shape, BF16),
        ),
        in_specs=[row_spec, row_spec, weight_spec],
        out_specs=(row_spec, row_spec, weight_spec),
        compiler_params=pltpu.CompilerParams(vmem_limit_bytes=VMEM_LIMIT),
        cost_estimate=pl.CostEstimate(
            flops=flops, bytes_accessed=4 * weights.size, transcendentals=0
        ),
        name="experts",
    )(slots, grads, weights)


def turned(values, axis_name, step):
    ways = lax.axis_size(axis_name)
    return lax.ppermute(values, axis_name, [((i + step) % ways, i) for i in range(ways)])


def flipped(values, axis_name, bit):
    ways = lax.axis_size(axis_name)
    return lax.ppermute(values, axis_name, [(i, i ^ (1 << bit)) for i in range(ways)])


def sum_everywhere(values, axis_names):
    for axis_name in axis_names:
        for bit in range(lax.axis_size(axis_name).bit_length() - 1):
            values = values + flipped(values, axis_name, bit)
    return values


def cyclic(values, me, ways, axis, direction):
    size = values.shape[axis] // ways
    return jnp.concatenate(
        [
            lax.dynamic_slice_in_dim(
                values, lax.rem(me + direction * r + ways, ways) * size, size, axis
            )
            for r in range(ways)
        ],
        axis=axis,
    )


def shards(
    tokens,
    routes,
    buckets,
    gain_attn,
    w_query,
    w_key,
    w_value,
    w_out,
    bias_table,
    gain_ff,
    router,
    expert_up,
    expert_down,
    out_grad,
):
    seq_count, block_rows, model_width = tokens.shape
    ways = lax.axis_size("seq")
    group = lax.axis_size("fsdp")
    me = lax.axis_index("seq")
    length = block_rows * ways
    capacity = block_rows * 9 // 16
    expert_count = router.shape[1]
    token_rows = seq_count * block_rows
    slot_rows = seq_count * capacity
    width = model_width // ways
    local_heads = width // HEAD
    places = jnp.full((1,), me, jnp.int32)

    inputs_all = jnp.concatenate([tokens] + [turned(tokens, "seq", r) for r in range(1, ways)], axis=1)

    def columns_of(place):
        return jnp.concatenate(
            [
                lax.dynamic_slice_in_dim(weight, place * width, width, 1)
                for weight in (w_query, w_key, w_value)
            ],
            axis=1,
        )

    own_columns = lax.all_gather(columns_of(me), "fsdp", axis=0, tiled=True)

    own_experts = jnp.stack([expert_up, expert_down])
    far_experts = flipped(own_experts, "seq", 1)
    expert_weights = lax.all_gather(jnp.stack([own_experts, far_experts]), "fsdp", axis=0)
    full_out = lax.all_gather(w_out, "fsdp", axis=0, tiled=True)
    out_cyclic = cyclic(full_out, me, ways, 0, -1)
    rest_columns = lax.all_gather(
        jnp.concatenate([columns_of(lax.rem(me - r + ways, ways)) for r in range(1, ways)], axis=1),
        "fsdp",
        axis=0,
        tiled=True,
    )

    chosen = routes[:, :, 0]
    picked = (chosen[:, :, None] == jnp.arange(expert_count)[None, None, :]).astype(F32)
    earlier = jnp.cumsum(picked, axis=1) - picked
    slot_number = jnp.sum(earlier * picked, axis=-1).astype(jnp.int32)
    slot_index = chosen * capacity + slot_number
    dispatch = (
        slot_index[:, None, :] == jnp.arange(expert_count * capacity)[None, :, None]
    ).reshape(seq_count, expert_count, capacity, block_rows)
    dispatch_low = dispatch.astype(BF16)

    def to_slots(values):
        placed = jnp.einsum("nect,ntd->encd", dispatch_low, values, preferred_element_type=F32)
        return placed.astype(BF16).reshape(expert_count, slot_rows, model_width)

    def from_slots(values):
        return jnp.einsum(
            "nect,encd->ntd",
            dispatch_low,
            values.astype(BF16).reshape(expert_count, seq_count, capacity, model_width),
            preferred_element_type=F32,
        )

    grad_slots = to_slots(out_grad)
    far_grad_slots = flipped(grad_slots, "seq", 0)

    table_here = lax.dynamic_slice_in_dim(bias_table, me * local_heads, local_heads, 1)
    bucket_table = (buckets[:, None] == jnp.arange(bias_table.shape[0])[None, :]).astype(F32)
    reversed_buckets = jnp.pad(bucket_table[::-1], ((0, 1), (0, 0)))
    reversed_bias = jnp.einsum(
        "uk,kh->hu", reversed_buckets, table_here * LOG2E, precision=PRECISE
    )
    tiles = bias_tiles(reversed_bias[:, None, :], block_rows, length * 2 - block_rows)

    wide_inputs = inputs_all.astype(F32)
    scale_all = norm_scale(wide_inputs)
    normed_all = (wide_inputs * scale_all * gain_attn).astype(BF16)
    qkv = jnp.einsum("ntd,de->nte", normed_all, own_columns, preferred_element_type=F32).astype(BF16)
    contexts, totals = attend(places, qkv, tiles)

    def block_of(values, r):
        return values[:, r * block_rows : (r + 1) * block_rows]

    context_tokens = jnp.concatenate(
        [block_of(contexts, 0)]
        + [turned(block_of(contexts, r), "seq", -r) for r in range(1, ways)],
        axis=2,
    )
    context_rows = context_tokens.reshape(token_rows, model_width)
    attn_branch = jnp.dot(context_rows, out_cyclic, preferred_element_type=F32)
    inputs = tokens.astype(F32)
    first_scale = norm_scale(inputs)
    hidden = inputs + attn_branch.reshape(seq_count, block_rows, model_width)
    second_scale = norm_scale(hidden)
    ffnorm = hidden * second_scale * gain_ff
    logits = jnp.einsum("std,de->ste", ffnorm, router, precision=PRECISE)
    route_probs = jax.nn.softmax(logits, axis=-1)
    gate_value = jnp.sum(route_probs * picked, axis=-1)

    slots = to_slots(ffnorm.astype(BF16))
    gate_slots = jnp.einsum(
        "nect->enc", jnp.where(dispatch, gate_value[:, None, None, :], 0.0)
    ).reshape(expert_count, slot_rows)
    far_slots = flipped(slots, "seq", 0)
    far_gate_slots = flipped(gate_slots, "seq", 0)
    all_slots = jnp.concatenate([slots, far_slots], axis=1)
    all_grad_slots = jnp.concatenate([grad_slots, far_grad_slots], axis=1).astype(F32)
    all_gates = jnp.concatenate([gate_slots, far_gate_slots], axis=1)
    gated_grads = (all_grad_slots * all_gates[:, :, None]).astype(BF16)
    returned, slot_back, weight_parts = experts(all_slots, gated_grads, expert_weights)
    gate_parts = jnp.sum(returned * all_grad_slots, axis=-1)
    gate_grad_slots = gate_parts[:, :slot_rows] + flipped(gate_parts[:, slot_rows:], "seq", 0)
    slot_sum = slot_back[:, :slot_rows] + flipped(
        slot_back[:, slot_rows:].astype(BF16), "seq", 0
    ).astype(F32)
    returned_sum = returned[:, :slot_rows] + flipped(
        returned[:, slot_rows:].astype(BF16), "seq", 0
    ).astype(F32)

    output = (hidden + gate_value[:, :, None] * from_slots(returned_sum)).astype(BF16)
    upstream = out_grad.astype(F32)
    gate_grad = jnp.sum(
        jnp.where(
            dispatch,
            gate_grad_slots.reshape(expert_count, seq_count, capacity).transpose(1, 0, 2)[..., None],
            0.0,
        ),
        axis=(1, 2),
    )
    logit_grad = gate_value[:, :, None] * (picked - route_probs) * gate_grad[:, :, None]
    ffnorm_grad = from_slots(slot_sum) + jnp.einsum(
        "ste,de->std", logit_grad, router, precision=PRECISE
    )
    router_grad = jnp.einsum("std,ste->de", ffnorm, logit_grad, precision=PRECISE)
    weighted = ffnorm_grad * gain_ff
    inner_sum = jnp.mean(weighted * hidden, axis=-1, keepdims=True)
    hidden_grad = (
        upstream + second_scale * weighted - hidden * (second_scale**3) * inner_sum
    )
    gain_ff_grad = jnp.sum(ffnorm_grad * hidden * second_scale, axis=(0, 1))
    branch_grad = hidden_grad.astype(BF16).reshape(token_rows, model_width)
    context_grad = dot_of(branch_grad, out_cyclic, 1, 1).astype(BF16)
    context_grad = context_grad.reshape(seq_count, block_rows, model_width)
    context_grads = jnp.concatenate(
        [context_grad[:, :, :width]]
        + [
            turned(context_grad[:, :, r * width : (r + 1) * width], "seq", r)
            for r in range(1, ways)
        ],
        axis=1,
    )
    out_weight_grad = cyclic(dot_of(context_rows, branch_grad, 0, 0).astype(BF16), me, ways, 0, -1)

    qkv_grads, offset_grads = attend_back(places, qkv, context_grads, totals, tiles, 2 * length)
    own_grads = [block_of(qkv_grads, 0)] + [
        turned(block_of(qkv_grads, r), "seq", -r) for r in range(1, ways)
    ]
    column_grad = jnp.einsum("ntd,nte->de", normed_all, qkv_grads, preferred_element_type=F32)
    gain_attn_part = jnp.sum(column_grad * own_columns.astype(F32), axis=1) / gain_attn
    column_share = lax.psum_scatter(
        column_grad.astype(BF16), "fsdp", scatter_dimension=0, tiled=True
    )
    own_grads = jnp.concatenate(own_grads, axis=2)
    all_columns = jnp.concatenate([own_columns, rest_columns], axis=1)
    normed_grad = jnp.einsum("nte,de->ntd", own_grads, all_columns, preferred_element_type=F32)
    weighted = normed_grad * gain_attn
    inner_sum = jnp.mean(weighted * inputs, axis=-1, keepdims=True)
    tokens_grad = (
        hidden_grad + first_scale * weighted - inputs * (first_scale**3) * inner_sum
    )

    table_part = jnp.einsum(
        "uk,hu->kh", reversed_buckets, jnp.sum(offset_grads, axis=(0, 2)), precision=PRECISE
    )
    table_full = lax.dynamic_update_slice_in_dim(
        jnp.zeros(bias_table.shape, F32), table_part, me * local_heads, 1
    )
    small = jnp.concatenate(
        [gain_attn_part, gain_ff_grad, router_grad.reshape(-1), table_full.reshape(-1)]
    )
    small = sum_everywhere(small, ("fsdp", "seq"))
    gain_attn_sum = small[:model_width]
    gain_ff_sum = small[model_width : 2 * model_width]
    router_sum = small[2 * model_width : 2 * model_width + router.size].reshape(router.shape)
    table_sum = small[2 * model_width + router.size :].reshape(bias_table.shape)

    units = expert_up.shape[1]
    expert_share = lax.psum_scatter(weight_parts, "fsdp", scatter_dimension=0, tiled=True)[0]
    expert_sum = expert_share[0].astype(F32) + flipped(expert_share[1], "seq", 1).astype(F32)
    out_share = lax.psum_scatter(out_weight_grad, "fsdp", scatter_dimension=0, tiled=True)
    out_shares = [out_share] + [turned(out_share, "seq", r) for r in range(1, ways)]
    out_sum = sum(share.astype(F32) for share in out_shares)
    column_shares = jnp.concatenate(
        [column_share] + [turned(column_share, "seq", r) for r in range(1, ways)], axis=1
    )
    column_shares = cyclic(column_shares, ways - me, ways, 1, 1).astype(F32)
    column_shares = column_shares.reshape(-1, ways, 3, width)
    attn_sums = [column_shares[:, :, kind].reshape(-1, model_width) for kind in range(3)]
    return (
        output,
        tokens_grad,
        gain_attn_sum,
        attn_sums[0],
        attn_sums[1],
        attn_sums[2],
        out_sum,
        table_sum,
        gain_ff_sum,
        router_sum,
        expert_sum[0],
        expert_sum[1],
    )


def solution(mesh):
    in_specs = (
        P("fsdp", "seq", None),
        P("fsdp", "seq", None),
        P(),
        P(),
        P("fsdp", None),
        P("fsdp", None),
        P("fsdp", None),
        P("fsdp", None),
        P(),
        P(),
        P(),
        P(None, ("seq", "fsdp"), None),
        P(None, ("seq", "fsdp"), None),
        P("fsdp", "seq", None),
    )
    out_specs = (
        P("fsdp", "seq", None),
        P("fsdp", "seq", None),
        P(),
        P("fsdp", None),
        P("fsdp", None),
        P("fsdp", None),
        P("fsdp", None),
        P(),
        P(),
        P(),
        P(None, ("seq", "fsdp"), None),
        P(None, ("seq", "fsdp"), None),
    )
    return jax.shard_map(shards, mesh=mesh, in_specs=in_specs, out_specs=out_specs, check_vma=False)
```

time: 1110 us -> 395 us (0.36)
  waiting for transfers between devices: 590 us -> 181 us
  local copies, waits for them, and re-layouts: 214 us -> 31 us
  blocking collectives: 81.3 us -> 12.6 us
  matrix products: 94.6 us -> 29.3 us
  Pallas kernels: 0 us -> 57.8 us
  other arithmetic: 71.7 us -> 19.6 us
  starting transfers between devices: 23.5 us -> 47.5 us
  loops' own time: 12.8 us -> 0 us
    unnamed x17 -> x7, waiting for transfers between devices: 250 us -> 1.28 us
    all_gather x8 -> x3, waiting for transfers between devices: 149 us -> 0.01 us  [the longest x1 0.01 us: shards(): full_out = lax.all_gather(w_out, 'fsdp', axis=0, tiled=True)]
    reduce_scatter x5 -> x1, waiting for transfers between devices: 170 us -> 37.3 us  [shards(): lax.psum_scatter(weight_parts, 'fsdp', scatter_dimension=0, tiled=True)[0]]
    ppermute x0 -> x31, waiting for transfers between devices: none -> 106 us  [the longest x13 69.7 us: flipped(): lax.ppermute(values, axis_name, [(i, i ^ 1 << bit) for i in range(ways)])]
    while x17 -> x0, local copies, waits for them, and re-layouts: 89.2 us -> none
    dot_general x36 -> x12, matrix products: 90.3 us -> 25.4 us  [the longest x2 4.72 us: from_slots(): jnp.einsum('nect,encd->ntd', dispatch_low, values.astype(BF16).reshape(ex...]
    pallas_call x0 -> x4, Pallas kernels: none -> 57.8 us  [the longest x1 24.1 us: attend_back(): pl.pallas_call(attend_back_kernel, grid=(seq_count,), out_shape=(jax.Shap...]
    reshape x12 -> x3, local copies, waits for them, and re-layouts: 49.9 us -> 0.34 us  [the longest x1 0.22 us: shards(): router_grad.reshape(-1)]
  transfers between devices with their start and end apart: 21 -> 37, of which waited for: 13 -> 18; matrix products, arithmetic and copies ran while one was open for 32% -> 20% of each run, Pallas kernels for 0% -> 15%
where the time goes in v1:
time: 395 us; the launch traced here: 393 us
  waiting for transfers between devices  181 us (46%)
  Pallas kernels  57.8 us (15%)
  starting transfers between devices  47.5 us (12%)
  local copies, waits for them, and re-layouts  31 us (8%)
  matrix products  29.3 us (7%)
  other arithmetic  19.6 us (5%)
  between operations  14.8 us (4%)
  blocking collectives  12.6 us (3%)
    ppermute x13, waiting for transfers between devices, flipped(): lax.ppermute(values, axis_name, [(i, i ^ 1 << bit) for i in range(ways)])  69.7 us
    reduce_scatter x1, waiting for transfers between devices, shards(): lax.psum_scatter(weight_parts, 'fsdp', scatter_dimension=0, tiled=True)[0]  37.3 us
    reduce_scatter x1, waiting for transfers between devices, shards(): lax.psum_scatter(out_weight_grad, 'fsdp', scatter_dimension=0, tiled=True)  36.5 us
    ppermute x18, waiting for transfers between devices, turned(): lax.ppermute(values, axis_name, [((i + step) % ways, i) for i in range(wa...  35.9 us
    pallas_call x1, Pallas kernels, attend_back(): pl.pallas_call(attend_back_kernel, grid=(seq_count,), out_shape=(jax.Shap...  24.1 us
    ppermute x18, starting transfers between devices, turned(): lax.ppermute(values, axis_name, [((i + step) % ways, i) for i in range(wa...  24.1 us
    ppermute x13, starting transfers between devices, flipped(): lax.ppermute(values, axis_name, [(i, i ^ 1 << bit) for i in range(ways)])  23.1 us
    pallas_call x1, Pallas kernels, experts(): pl.pallas_call(experts_kernel, grid=(expert_count, groups), out_shape=(ja...  16.1 us
  transfers between devices with their start and end apart: 37, of which 18 were waited for; matrix products, arithmetic and copies ran while one was open for 20% of the time, Pallas kernels for 15%

profile of v1, /device:TPU:0, one launch (start us, length us, event | category | flops | bytes accessed | tf_op | source)
XLA Modules:
  0.0 393.4 jit_solution(14782335103816764716)
XLA Ops:
  8.0 1.1 fusion.80
  9.1 4.1 %collective-permute-start.9 = (bf16[2,2,96,768]{3,2,1,0:T(8,128)(2,1)S(1)}, bf16[2,2,96,768]{3,2,1,0:T(8,128)(2,1)S(1)}, u32[]{:S(2)}, u32[]{:S(2)}) collective-permute-start(bf16[2,2,96,768]{3,2,1,0:T(8,128)(2,1)S(1)} %get-tuple-element.92), channel_id=1, source_target_pairs={{0,16},{8,24},{16,0},{24,8},{1,17},{9,25},{17,1},{25,9},{2,18},{10... | collective-permute-start | bytes 1769480 | tf_op jit(solution)/shard_map/ppermute | solution.py:285
  13.2 26.0 %collective-permute-done.9 = bf16[2,2,96,768]{3,2,1,0:T(8,128)(2,1)S(1)} collective-permute-done((bf16[2,2,96,768]{3,2,1,0:T(8,128)(2,1)S(1)}, bf16[2,2,96,768]{3,2,1,0:T(8,128)(2,1)S(1)}, u32[]{:S(2)}, u32[]{:S(2)}) %collective-permute-start.9) | collective-permute-done | bytes 589856 | tf_op jit(solution)/shard_map/ppermute | solution.py:285
  40.4 3.6 collective-permute-start
  46.1 2.9 collective-permute-start.7
  51.8 1.6 fusion.23
  54.1 4.0 %bias_tiles.1.tiles_ref = f32[3,256,1792]{2,1,0:T(8,128)} custom-call(f32[3,1,2048]{2,1,0:T(1,128)} %broadcast_in_dim.27.reversed_ref), custom_call_target="tpu_custom_call" | custom-call | tf_op jit(solution)/shard_map/bias_tiles/pallas_call | solution.py:41
  58.1 12.6 %all_gather.15 = bf16[768,576]{1,0:T(8,128)(2,1)S(1)} all-gather(bf16[96,576]{1,0:T(8,128)(2,1)S(1)} %pad_maximum_fusion.10), channel_id=1, replica_groups=mesh['seq'=4,'fsdp'=8] {'fsdp'}, dimensions={0}, use_global_device_ids=true | all-gather | bytes 995328 | tf_op jit(solution)/shard_map/all_gather | solution.py:348
  70.8 6.4 %collective-permute-done.1 = bf16[1,256,768]{2,1,0:T(8,128)(2,1)} collective-permute-done((bf16[1,256,768]{2,1,0:T(8,128)(2,1)S(1)}, bf16[1,256,768]{2,1,0:T(8,128)(2,1)}, u32[]{:S(2)}, u32[]{:S(2)}) %collective-permute-start.1) | collective-permute-done | bytes 393248 | tf_op jit(solution)/shard_map/ppermute | solution.py:280
  77.1 1.6 multiply_reduce_fusion
  78.8 3.8 fusion.6.qkv_ref
  82.6 13.6 %attend.1 = (bf16[1,1024,192]{2,1,0:T(8,128)(2,1)}, f32[1,3,1,1024]{3,2,1,0:T(1,128)}) custom-call(s32[1]{0:T(128)} %bitcast.me_ref, bf16[1,1024,576]{2,1,0:T(8,128)(2,1)} %fusion.6.qkv_ref, f32[3,256,1792]{2,1,0:T(8,128)} %bias_tiles.1.tiles_ref), custom_call_target="tpu_custom_call" | custom-call | tf_op jit(solution)/shard_map/attend/pallas_call | solution.py:102
  96.2 1.2 fusion.85
  97.4 1.4 collective-permute-start.3
  98.8 2.1 collective-permute-start.4
  100.9 2.8 collective-permute-start.5
  103.8 1.3 constant_dynamic-slice_fusion.20
  105.3 4.6 %collective-permute-done.4 = bf16[1,256,192]{2,1,0:T(8,128)(2,1)S(1)} collective-permute-done((bf16[1,256,192]{2,1,0:T(8,128)(2,1)S(1)}, bf16[1,256,192]{2,1,0:T(8,128)(2,1)S(1)}, u32[]{:S(2)}, u32[]{:S(2)}) %collective-permute-start.4) | collective-permute-done | bytes 98336 | tf_op jit(solution)/shard_map/ppermute | solution.py:280
  110.6 1.6 multiply_reduce_fusion.2
  113.6 2.8 collective-permute-start.6
  116.7 9.7 %collective-permute-done.8 = f32[2,144]{1,0:T(2,128)S(1)} collective-permute-done((f32[2,144]{1,0:T(2,128)S(1)}, f32[2,144]{1,0:T(2,128)S(1)}, u32[]{:S(2)}, u32[]{:S(2)}) %collective-permute-start.8) | collective-permute-done | bytes 1184 | tf_op jit(solution)/shard_map/ppermute | solution.py:285
  126.5 2.2 fusion.4.grads_ref
  128.6 2.0 pad_maximum_fusion.3.slots_ref
  130.7 16.1 %experts.1 = (f32[2,288,768]{2,1,0:T(8,128)}, f32[2,288,768]{2,1,0:T(8,128)}, bf16[8,2,2,2,96,768]{5,4,3,2,1,0:T(8,128)(2,1)}) custom-call(bf16[2,288,768]{2,1,0:T(8,128)(2,1)} %pad_maximum_fusion.3.slots_ref, bf16[2,288,768]{2,1,0:T(8,128)(2,1)} %fusion.4.grads_ref, bf16[8,2,2,2,96,768]{5,4,3,2,1,0:T(8,128)(2,1)} %bitcast.153), custom_call_target="tpu_custom_call" | custom-call | flops 8153726976 | bytes 18874368 | tf_op jit(solution)/shard_map/experts/pallas_call | solution.py:260
  146.8 1.8 fusion.5
  148.7 1.7 collective-permute-start.12
  150.4 1.2 slice.185
  153.4 8.8 %collective-permute-done.11 = bf16[2,144,768]{2,1,0:T(8,128)(2,1)S(1)} collective-permute-done((bf16[2,144,768]{2,1,0:T(8,128)(2,1)S(1)}, bf16[2,144,768]{2,1,0:T(8,128)(2,1)S(1)}, u32[]{:S(2)}, u32[]{:S(2)}) %collective-permute-start.11) | collective-permute-done | bytes 442400 | tf_op jit(solution)/shard_map/ppermute | solution.py:285
  162.2 2.4 fusion.30
  167.2 1.2 collective-permute-start.13
  170.4 2.2 copy.53
  172.6 1.9 collective-permute-done.13
  174.6 4.5 %collective-permute-done.14 = bf16[1,256,192]{2,1,0:T(8,128)(2,1)S(1)} collective-permute-done((bf16[1,256,192]{2,1,0:T(8,128)(2,1)}, bf16[1,256,192]{2,1,0:T(8,128)(2,1)S(1)}, u32[]{:S(2)}, u32[]{:S(2)}) %collective-permute-start.14) | collective-permute-done | bytes 98336 | tf_op jit(solution)/shard_map/ppermute | solution.py:280
  179.1 1.8 pad_maximum_fusion.7.grad_ref
  180.9 24.1 %attend_back.1 = (bf16[1,1024,576]{2,1,0:T(8,128)(2,1)}, f32[1,3,1,2048]{3,2,1,0:T(1,128)}) custom-call(s32[1]{0:T(128)} %bitcast.me_ref, bf16[1,1024,576]{2,1,0:T(8,128)(2,1)} %fusion.6.qkv_ref, bf16[1,1024,192]{2,1,0:T(8,128)(2,1)} %pad_maximum_fusion.7.grad_ref, f32[1,3,1,1024]{3,2,1,0:T(1,128)} %get-tuple-element.22.total_ref, ...), custom_call_target="tpu_custom_call" | custom-call | tf_op jit(solution)/shard_map/attend_back/pallas_call | solution.py:191
  205.0 4.5 %fusion.82 = (bf16[768,576]{0,1:T(8,128)(2,1)}, f32[768]{0:T(1024)}) fusion(bf16[768,576]{0,1:T(8,128)(2,1)S(1)} %copy-done.10, bf16[1,1024,576]{2,1,0:T(8,128)(2,1)} %get-tuple-element.23, bf16[256,768]{1,0:T(8,128)(2,1)} %bitcast.4, bf16[256,768]{1,0:T(8,128)(2,1)} %bitcast.3, bf16[256,768]{1,0:T(8,128)(2,1)} %bitcast.2, ...), kind=kOutput, calls=%fused_computation.171 | convolution fusion | flops 916389120 | bytes 4532224 | tf_op jit(solution)/shard_map/ntd,nte->de/dot_general | solution.py:478
  209.6 2.2 copy.64
  212.5 2.0 slice.186
  214.5 2.2 fusion.33
  217.6 2.5 fusion.21
  221.2 1.7 convolution_convert_fusion.1
  222.9 2.0 collective-permute-start.20
  225.0 1.7 collective-permute-done.20
  226.7 2.5 collective-permute-start.21
  229.3 1.1 pad_maximum_fusion.2
  231.0 2.1 collective-permute-start.22
  233.1 2.2 fusion.83
  236.1 3.1 collective-permute-start.18
  239.2 2.1 collective-permute-start.23
  241.3 2.3 fusion.16
  243.6 22.7 %collective-permute-done.23 = f32[3456]{0:T(1024)S(1)} collective-permute-done((f32[3456]{0:T(1024)S(1)}, f32[3456]{0:T(1024)S(1)}, u32[]{:S(2)}, u32[]{:S(2)}) %collective-permute-start.23) | collective-permute-done | bytes 13856 | tf_op jit(solution)/shard_map/ppermute | solution.py:285
  268.8 3.3 concatenate.89
  272.2 3.7 fusion.25
  277.7 1.4 collective-permute-start.26
  279.1 1.1 fusion.27
  280.2 3.2 collective-permute-done.24
  283.4 6.0 %collective-permute-done.25 = bf16[96,576]{0,1:T(8,128)(2,1)S(1)} collective-permute-done((bf16[96,576]{0,1:T(8,128)(2,1)S(1)}, bf16[96,576]{0,1:T(8,128)(2,1)S(1)}, u32[]{:S(2)}, u32[]{:S(2)}) %collective-permute-start.25) | collective-permute-done | bytes 110624 | tf_op jit(solution)/shard_map/ppermute | solution.py:280
  289.6 37.3 %reduce-scatter.8.cloned.1.call-done = bf16[1,2,2,2,96,768]{5,4,3,2,1,0:T(8,128)(2,1)} async-done(((bf16[8,2,2,2,96,768]{5,4,3,2,1,0:T(8,128)(2,1)}), bf16[1,2,2,2,96,768]{5,4,3,2,1,0:T(8,128)(2,1)}) %reduce-scatter.8.cloned.1.call-update) | async-done | bytes 1179664 | tf_op jit(solution)/shard_map/reduce_scatter | solution.py:508
  328.0 2.5 collective-permute-start.30
  330.7 36.5 %reduce-scatter.6.cloned.1.call-done = bf16[96,768]{1,0:T(8,128)(2,1)} async-done(((bf16[768,768]{1,0:T(8,128)(2,1)}), bf16[96,768]{1,0:T(8,128)(2,1)}) %reduce-scatter.6.cloned.1.call-update) | async-done | bytes 147472 | tf_op jit(solution)/shard_map/reduce_scatter | solution.py:510
  367.2 3.3 collective-permute-start.27
  370.5 1.1 collective-permute-start.29
  375.1 8.3 %collective-permute-done.28 = bf16[96,768]{1,0:T(8,128)(2,1)} collective-permute-done((bf16[96,768]{1,0:T(8,128)(2,1)}, bf16[96,768]{1,0:T(8,128)(2,1)}, u32[]{:S(2)}, u32[]{:S(2)}) %collective-permute-start.28) | collective-permute-done | bytes 147488 | tf_op jit(solution)/shard_map/ppermute | solution.py:280
  383.4 1.9 convert_add_fusion.2
  (211 shorter events, 30.9 us)
Async XLA Ops:
  7.2 105.5 %copy-start = (f32[768,2]{0,1:T(2,128)S(1)}, f32[768,2]{0,1:T(2,128)}, u32[]{:S(2)}) copy-start(f32[768,2]{0,1:T(2,128)} %param.24) | copy-start | bytes 18436
  7.2 96.6 %all-gather.5.cloned.1.call-start = ((), (), s32[]{:S(2)}) async-start(), calls=%async_computation.3 | async-start | bytes 1327104 | tf_op jit(solution)/shard_map/all_gather | solution.py:353
  7.9 122.7 %all-gather.9.cloned.1.call-start = ((), (), s32[]{:S(2)}) async-start(), calls=%async_computation.7 | async-start | bytes 10616832 | tf_op jit(solution)/shard_map/all_gather | solution.py:352
  9.1 30.1 %collective-permute-start.9 = (bf16[2,2,96,768]{3,2,1,0:T(8,128)(2,1)S(1)}, bf16[2,2,96,768]{3,2,1,0:T(8,128)(2,1)S(1)}, u32[]{:S(2)}, u32[]{:S(2)}) collective-permute-start(bf16[2,2,96,768]{3,2,1,0:T(8,128)(2,1)S(1)} %get-tuple-element.92), channel_id=1, source_target_pairs={{0,16},{8,24},{16,0},{24,8},{1,17},{9,25},{17,1},{25,9},{2,18},{10... | collective-permute-start | bytes 1769480 | tf_op jit(solution)/shard_map/ppermute | solution.py:285
  39.2 9.8 %copy-start.20 = (bf16[96,768]{1,0:T(8,128)(2,1)S(1)}, bf16[96,768]{1,0:T(8,128)(2,1)}, u32[]{:S(2)}) copy-start(bf16[96,768]{1,0:T(8,128)(2,1)} %param.18) | copy-start | bytes 442372
  40.3 8.9 %copy-start.21 = (bf16[96,768]{1,0:T(8,128)(2,1)S(1)}, bf16[96,768]{1,0:T(8,128)(2,1)}, u32[]{:S(2)}) copy-start(bf16[96,768]{1,0:T(8,128)(2,1)} %param.20) | copy-start | bytes 442372
  40.3 8.9 %copy-start.22 = (bf16[96,768]{1,0:T(8,128)(2,1)S(1)}, bf16[96,768]{1,0:T(8,128)(2,1)}, u32[]{:S(2)}) copy-start(bf16[96,768]{1,0:T(8,128)(2,1)} %param.19) | copy-start | bytes 442372
  40.3 10.1 %copy-start.40 = (s32[2047]{0:T(1024)S(1)}, s32[2047]{0:T(1024)}, u32[]{:S(2)}) copy-start(s32[2047]{0:T(1024)} %param.16) | copy-start | bytes 24568
  40.3 231.8 %all-gather.7.cloned.1.call-start = ((), (), s32[]{:S(2)}) async-start(), calls=%async_computation.4 | async-start | bytes 3096576 | tf_op jit(solution)/shard_map/all_gather | solution.py:355
  40.4 30.4 %collective-permute-start = (bf16[1,256,768]{2,1,0:T(8,128)(2,1)S(1)}, bf16[1,256,768]{2,1,0:T(8,128)(2,1)}, u32[]{:S(2)}, u32[]{:S(2)}) collective-permute-start(bf16[1,256,768]{2,1,0:T(8,128)(2,1)S(1)} %copy-done.7), channel_id=1, source_target_pairs={{8,0},{16,8},{24,16},{0,24},{9,1},{17,9},{25,17},{1,25},{10,2},{18... | collective-permute-start | bytes 1179656 | tf_op jit(solution)/shard_map/ppermute | solution.py:280
  44.0 33.1 %collective-permute-start.1 = (bf16[1,256,768]{2,1,0:T(8,128)(2,1)S(1)}, bf16[1,256,768]{2,1,0:T(8,128)(2,1)}, u32[]{:S(2)}, u32[]{:S(2)}) collective-permute-start(bf16[1,256,768]{2,1,0:T(8,128)(2,1)S(1)} %copy-done.7), channel_id=1, source_target_pairs={{16,0},{24,8},{0,16},{8,24},{17,1},{25,9},{1,17},{9,25},{18,2},{26... | collective-permute-start | bytes 1179656 | tf_op jit(solution)/shard_map/ppermute | solution.py:280
  44.0 33.1 %collective-permute-start.2 = (bf16[1,256,768]{2,1,0:T(8,128)(2,1)S(1)}, bf16[1,256,768]{2,1,0:T(8,128)(2,1)}, u32[]{:S(2)}, u32[]{:S(2)}) collective-permute-start(bf16[1,256,768]{2,1,0:T(8,128)(2,1)S(1)} %copy-done.7), channel_id=1, source_target_pairs={{24,0},{0,8},{8,16},{16,24},{25,1},{1,9},{9,17},{17,25},{26,2},{2,... | collective-permute-start | bytes 1179656 | tf_op jit(solution)/shard_map/ppermute | solution.py:280
  46.1 80.4 %collective-permute-start.7 = (bf16[2,144,768]{2,1,0:T(8,128)(2,1)S(1)}, bf16[2,144,768]{2,1,0:T(8,128)(2,1)}, u32[]{:S(2)}, u32[]{:S(2)}) collective-permute-start(bf16[2,144,768]{2,1,0:T(8,128)(2,1)S(1)} %convolution_convert_fusion.2), channel_id=1, source_target_pairs={{0,8},{8,0},{16,24},{24,16},{1,9},{9,1},{17,25},{25,17},{2,10},{10... | collective-permute-start | bytes 1327112 | tf_op jit(solution)/shard_map/ppermute | solution.py:285
  50.3 225.6 %reduce-scatter.10.cloned.1.call-start = ((), (), s32[]{:S(2)}) async-start(), calls=%async_computation.8 | async-start | bytes 1105920
  58.0 20.7 %copy-start.41 = (f32[768]{0:T(1024)S(1)}, f32[768]{0:T(1024)}, u32[]{:S(2)}) copy-start(f32[768]{0:T(1024)} %param.17) | copy-start | bytes 9220
  70.8 11.8 %copy-start.3 = (bf16[768,576]{1,0:T(8,128)(2,1)}, bf16[768,576]{1,0:T(8,128)(2,1)S(1)}, u32[]{:S(2)}) copy-start(bf16[768,576]{1,0:T(8,128)(2,1)S(1)} %all_gather.15) | copy-start | bytes 2654212
  96.2 14.4 %copy-start.8 = (bf16[1,256,768]{2,1,0:T(8,128)(2,1)S(1)}, bf16[1,256,768]{2,1,0:T(8,128)(2,1)}, u32[]{:S(2)}) copy-start(bf16[1,256,768]{2,1,0:T(8,128)(2,1)} %param.14) | copy-start | bytes 1179652
  97.4 7.9 %collective-permute-start.3 = (bf16[1,256,192]{2,1,0:T(8,128)(2,1)S(1)}, bf16[1,256,192]{2,1,0:T(8,128)(2,1)S(1)}, u32[]{:S(2)}, u32[]{:S(2)}) collective-permute-start(bf16[1,256,192]{2,1,0:T(8,128)(2,1)S(1)} %get-tuple-element.96), channel_id=1, source_target_pairs={{24,0},{0,8},{8,16},{16,24},{25,1},{1,9},{9,17},{17,25},{26,2},{2,... | collective-permute-start | bytes 294920 | tf_op jit(solution)/shard_map/ppermute | solution.py:280
  98.8 11.1 %collective-permute-start.4 = (bf16[1,256,192]{2,1,0:T(8,128)(2,1)S(1)}, bf16[1,256,192]{2,1,0:T(8,128)(2,1)S(1)}, u32[]{:S(2)}, u32[]{:S(2)}) collective-permute-start(bf16[1,256,192]{2,1,0:T(8,128)(2,1)S(1)} %get-tuple-element.95), channel_id=1, source_target_pairs={{16,0},{24,8},{0,16},{8,24},{17,1},{25,9},{1,17},{9,25},{18,2},{26... | collective-permute-start | bytes 294920 | tf_op jit(solution)/shard_map/ppermute | solution.py:280
  100.9 9.0 %collective-permute-start.5 = (bf16[1,256,192]{2,1,0:T(8,128)(2,1)S(1)}, bf16[1,256,192]{2,1,0:T(8,128)(2,1)S(1)}, u32[]{:S(2)}, u32[]{:S(2)}) collective-permute-start(bf16[1,256,192]{2,1,0:T(8,128)(2,1)S(1)} %get-tuple-element.94), channel_id=1, source_target_pairs={{8,0},{16,8},{24,16},{0,24},{9,1},{17,9},{25,17},{1,25},{10,2},{18... | collective-permute-start | bytes 294920 | tf_op jit(solution)/shard_map/ppermute | solution.py:280
  105.1 7.1 %copy-start.12 = (bf16[192,768]{1,0:T(8,128)(2,1)}, bf16[192,768]{1,0:T(8,128)(2,1)S(1)}, u32[]{:S(2)}) copy-start(bf16[192,768]{1,0:T(8,128)(2,1)S(1)} %get-tuple-element.83) | copy-start | bytes 884740
  105.1 7.1 %copy-start.14 = (bf16[192,768]{1,0:T(8,128)(2,1)}, bf16[192,768]{1,0:T(8,128)(2,1)S(1)}, u32[]{:S(2)}) copy-start(bf16[192,768]{1,0:T(8,128)(2,1)S(1)} %get-tuple-element.84) | copy-start | bytes 884740
  105.1 7.1 %copy-start.16 = (bf16[192,768]{1,0:T(8,128)(2,1)}, bf16[192,768]{1,0:T(8,128)(2,1)S(1)}, u32[]{:S(2)}) copy-start(bf16[192,768]{1,0:T(8,128)(2,1)S(1)} %get-tuple-element.85) | copy-start | bytes 884740
  105.1 7.1 %copy-start.18 = (bf16[192,768]{1,0:T(8,128)(2,1)}, bf16[192,768]{1,0:T(8,128)(2,1)S(1)}, u32[]{:S(2)}) copy-start(bf16[192,768]{1,0:T(8,128)(2,1)S(1)} %get-tuple-element.86) | copy-start | bytes 884740
  112.3 52.3 %copy-start.30 = (f32[256]{0:T(256)}, f32[256]{0:T(256)S(1)}, u32[]{:S(2)}) copy-start(f32[256]{0:T(256)S(1)} %get-tuple-element.118) | copy-start | bytes 3076
  113.6 15.1 %collective-permute-start.6 = (bf16[2,144,768]{2,1,0:T(8,128)(2,1)S(1)}, bf16[2,144,768]{2,1,0:T(8,128)(2,1)}, u32[]{:S(2)}, u32[]{:S(2)}) collective-permute-start(bf16[2,144,768]{2,1,0:T(8,128)(2,1)S(1)} %fusion.17), channel_id=1, source_target_pairs={{0,8},{8,0},{16,24},{24,16},{1,9},{9,1},{17,25},{25,17},{2,10},{10... | collective-permute-start | bytes 1327112 | tf_op jit(solution)/shard_map/ppermute | solution.py:285
  116.4 36.1 %copy-start.36 = (f32[256]{0:T(256)}, f32[256]{0:T(256)S(1)}, u32[]{:S(2)}) copy-start(f32[256]{0:T(256)S(1)} %get-tuple-element.66) | copy-start | bytes 3076
  116.5 36.1 %copy-start.38 = (f32[256,2]{0,1:T(2,128)}, f32[256,2]{0,1:T(2,128)S(1)}, u32[]{:S(2)}) copy-start(f32[256,2]{0,1:T(2,128)S(1)} %get-tuple-element.67) | copy-start | bytes 6148
  116.7 9.7 %collective-permute-start.8 = (f32[2,144]{1,0:T(2,128)S(1)}, f32[2,144]{1,0:T(2,128)S(1)}, u32[]{:S(2)}, u32[]{:S(2)}) collective-permute-start(f32[2,144]{1,0:T(2,128)S(1)} %transpose.56), channel_id=1, source_target_pairs={{0,8},{8,0},{16,24},{24,16},{1,9},{9,1},{17,25},{25,17},{2,10},{10... | collective-permute-start | bytes 3464 | tf_op jit(solution)/shard_map/ppermute | solution.py:285
  148.7 3.6 collective-permute-start.12
  151.6 10.5 %collective-permute-start.11 = (bf16[2,144,768]{2,1,0:T(8,128)(2,1)S(1)}, bf16[2,144,768]{2,1,0:T(8,128)(2,1)S(1)}, u32[]{:S(2)}, u32[]{:S(2)}) collective-permute-start(bf16[2,144,768]{2,1,0:T(8,128)(2,1)S(1)} %slice.185), channel_id=1, source_target_pairs={{0,8},{8,0},{16,24},{24,16},{1,9},{9,1},{17,25},{25,17},{2,10},{10... | collective-permute-start | bytes 1327112 | tf_op jit(solution)/shard_map/ppermute | solution.py:285
  152.5 12.1 %copy-start.39 = (f32[256]{0:T(256)}, f32[256]{0:T(256)S(1)}, u32[]{:S(2)}) copy-start(f32[256]{0:T(256)S(1)} %select_reduce_fusion) | copy-start | bytes 3076
  153.4 11.2 %copy-start.6 = (bf16[1,256,768]{2,1,0:T(8,128)(2,1)S(1)}, bf16[1,256,768]{2,1,0:T(8,128)(2,1)}, u32[]{:S(2)}) copy-start(bf16[1,256,768]{2,1,0:T(8,128)(2,1)} %param.27) | copy-start | bytes 1179652
  167.2 11.9 %copy-start.11 = (bf16[1,256,192]{2,1,0:T(8,128)(2,1)S(1)}, bf16[1,256,192]{2,1,0:T(8,128)(2,1)}, u32[]{:S(2)}) copy-start(bf16[1,256,192]{2,1,0:T(8,128)(2,1)} %get-tuple-element.97) | copy-start | bytes 294916
  167.2 7.3 %collective-permute-start.13 = (bf16[1,256,192]{2,1,0:T(8,128)(2,1)}, bf16[1,256,192]{2,1,0:T(8,128)(2,1)S(1)}, u32[]{:S(2)}, u32[]{:S(2)}) collective-permute-start(bf16[1,256,192]{2,1,0:T(8,128)(2,1)} %get-tuple-element.100), channel_id=1, source_target_pairs={{8,0},{16,8},{24,16},{0,24},{9,1},{17,9},{25,17},{1,25},{10,2},{18... | collective-permute-start | bytes 294920 | tf_op jit(solution)/shard_map/ppermute | solution.py:280
  168.4 10.7 %collective-permute-start.14 = (bf16[1,256,192]{2,1,0:T(8,128)(2,1)}, bf16[1,256,192]{2,1,0:T(8,128)(2,1)S(1)}, u32[]{:S(2)}, u32[]{:S(2)}) collective-permute-start(bf16[1,256,192]{2,1,0:T(8,128)(2,1)} %get-tuple-element.99), channel_id=1, source_target_pairs={{16,0},{24,8},{0,16},{8,24},{17,1},{25,9},{1,17},{9,25},{18,2},{26... | collective-permute-start | bytes 294920 | tf_op jit(solution)/shard_map/ppermute | solution.py:280
  169.3 9.8 %collective-permute-start.15 = (bf16[1,256,192]{2,1,0:T(8,128)(2,1)}, bf16[1,256,192]{2,1,0:T(8,128)(2,1)}, u32[]{:S(2)}, u32[]{:S(2)}) collective-permute-start(bf16[1,256,192]{2,1,0:T(8,128)(2,1)} %get-tuple-element.98), channel_id=1, source_target_pairs={{24,0},{0,8},{8,16},{16,24},{25,1},{1,9},{9,17},{17,25},{26,2},{2,... | collective-permute-start | bytes 294920 | tf_op jit(solution)/shard_map/ppermute | solution.py:280
  180.9 24.1 %copy-start.10 = (bf16[768,576]{0,1:T(8,128)(2,1)S(1)}, bf16[768,576]{0,1:T(8,128)(2,1)}, u32[]{:S(2)}) copy-start(bf16[768,576]{0,1:T(8,128)(2,1)} %copy.53) | copy-start | bytes 2654212
  180.9 24.1 %copy-start.42 = (f32[768]{0:T(1024)S(1)}, f32[768]{0:T(1024)}, u32[]{:S(2)}) copy-start(f32[768]{0:T(1024)} %param.17) | copy-start | bytes 9220
  180.9 24.1 %copy-start.45 = (f32[1024]{0:T(1024)S(1)}, f32[1024]{0:T(1024)}, u32[]{:S(2)}) copy-start(f32[1024]{0:T(1024)} %copy-done.44) | copy-start | bytes 12292
  211.8 115.1 %reduce-scatter.8.cloned.1.call-start = ((), (), s32[]{:S(2)}) async-start(), calls=%async_computation.6 | async-start | bytes 10616832 | tf_op jit(solution)/shard_map/reduce_scatter | solution.py:508
  212.4 154.8 %reduce-scatter.6.cloned.1.call-start = ((), (), s32[]{:S(2)}) async-start(), calls=%async_computation.5 | async-start | bytes 1327104 | tf_op jit(solution)/shard_map/reduce_scatter | solution.py:510
  214.5 26.8 %collective-permute-start.10 = (bf16[2,144,768]{2,1,0:T(8,128)(2,1)}, bf16[2,144,768]{2,1,0:T(8,128)(2,1)}, u32[]{:S(2)}, u32[]{:S(2)}) collective-permute-start(bf16[2,144,768]{2,1,0:T(8,128)(2,1)} %slice.186), channel_id=1, source_target_pairs={{0,8},{8,0},{16,24},{24,16},{1,9},{9,1},{17,25},{25,17},{2,10},{10... | collective-permute-start | bytes 1327112 | tf_op jit(solution)/shard_map/ppermute | solution.py:285
  221.2 1.7 collective-permute-start.19
  222.9 3.8 collective-permute-start.20
  226.7 4.2 %collective-permute-start.21 = (f32[3456]{0:T(1024)S(1)}, f32[3456]{0:T(1024)S(1)}, u32[]{:S(2)}, u32[]{:S(2)}) collective-permute-start(f32[3456]{0:T(1024)S(1)} %add.243), channel_id=1, source_target_pairs={{0,4},{1,5},{2,6},{3,7},{4,0},{5,1},{6,2},{7,3},{8,12},{9,13},{10,... | collective-permute-start | bytes 41480 | tf_op jit(solution)/shard_map/ppermute | solution.py:285
  230.4 10.9 %copy-start.29 = (s32[256]{0:T(256)S(1)}, s32[256]{0:T(256)}, u32[]{:S(2)}) copy-start(s32[256]{0:T(256)} %copy-done.27) | copy-start | bytes 3076
  230.4 10.9 %copy-start.37 = (f32[256]{0:T(256)S(1)}, f32[256]{0:T(256)}, u32[]{:S(2)}) copy-start(f32[256]{0:T(256)} %copy-done.36) | copy-start | bytes 3076
  230.4 10.8 %copy-start.2 = (f32[2,288,768]{2,1,0:T(8,128)S(1)}, f32[2,288,768]{2,1,0:T(8,128)}, u32[]{:S(2)}) copy-start(f32[2,288,768]{2,1,0:T(8,128)} %get-tuple-element.20) | copy-start | bytes 5308420
  231.0 8.2 %collective-permute-start.22 = (f32[3456]{0:T(1024)S(1)}, f32[3456]{0:T(1024)S(1)}, u32[]{:S(2)}, u32[]{:S(2)}) collective-permute-start(f32[3456]{0:T(1024)S(1)} %add.244), channel_id=1, source_target_pairs={{0,8},{8,0},{16,24},{24,16},{1,9},{9,1},{17,25},{25,17},{2,10},{10... | collective-permute-start | bytes 41480 | tf_op jit(solution)/shard_map/ppermute | solution.py:285
  235.3 33.5 %collective-permute-start.16 = (bf16[1,256,576]{2,1,0:T(8,128)(2,1)}, bf16[1,256,576]{2,1,0:T(8,128)(2,1)}, u32[]{:S(2)}, u32[]{:S(2)}) collective-permute-start(bf16[1,256,576]{2,1,0:T(8,128)(2,1)} %get-tuple-element.72), channel_id=1, source_target_pairs={{24,0},{0,8},{8,16},{16,24},{25,1},{1,9},{9,17},{17,25},{26,2},{2,... | collective-permute-start | bytes 884744 | tf_op jit(solution)/shard_map/ppermute | solution.py:280
  235.3 33.5 %collective-permute-start.17 = (bf16[1,256,576]{2,1,0:T(8,128)(2,1)}, bf16[1,256,576]{2,1,0:T(8,128)(2,1)}, u32[]{:S(2)}, u32[]{:S(2)}) collective-permute-start(bf16[1,256,576]{2,1,0:T(8,128)(2,1)} %get-tuple-element.71), channel_id=1, source_target_pairs={{16,0},{24,8},{0,16},{8,24},{17,1},{25,9},{1,17},{9,25},{18,2},{26... | collective-permute-start | bytes 884744 | tf_op jit(solution)/shard_map/ppermute | solution.py:280
  236.1 32.7 %collective-permute-start.18 = (bf16[1,256,576]{2,1,0:T(8,128)(2,1)S(1)}, bf16[1,256,576]{2,1,0:T(8,128)(2,1)}, u32[]{:S(2)}, u32[]{:S(2)}) collective-permute-start(bf16[1,256,576]{2,1,0:T(8,128)(2,1)S(1)} %get-tuple-element.70), channel_id=1, source_target_pairs={{8,0},{16,8},{24,16},{0,24},{9,1},{17,9},{25,17},{1,25},{10,2},{18... | collective-permute-start | bytes 884744 | tf_op jit(solution)/shard_map/ppermute | solution.py:280
  239.2 27.1 %collective-permute-start.23 = (f32[3456]{0:T(1024)S(1)}, f32[3456]{0:T(1024)S(1)}, u32[]{:S(2)}, u32[]{:S(2)}) collective-permute-start(f32[3456]{0:T(1024)S(1)} %add.245), channel_id=1, source_target_pairs={{0,16},{8,24},{16,0},{24,8},{1,17},{9,25},{17,1},{25,9},{2,18},{10... | collective-permute-start | bytes 41480 | tf_op jit(solution)/shard_map/ppermute | solution.py:285
  243.6 28.6 %copy-start.4 = (bf16[768,576]{1,0:T(8,128)(2,1)S(1)}, bf16[768,576]{1,0:T(8,128)(2,1)}, u32[]{:S(2)}) copy-start(bf16[768,576]{1,0:T(8,128)(2,1)} %copy-done.3) | copy-start | bytes 2654212
  243.6 28.6 %copy-start.43 = (f32[768]{0:T(1024)S(1)}, f32[768]{0:T(1024)}, u32[]{:S(2)}) copy-start(f32[768]{0:T(1024)} %param.17) | copy-start | bytes 9220
  277.0 6.4 %collective-permute-start.24 = (bf16[96,576]{0,1:T(8,128)(2,1)S(1)}, bf16[96,576]{0,1:T(8,128)(2,1)S(1)}, u32[]{:S(2)}, u32[]{:S(2)}) collective-permute-start(bf16[96,576]{0,1:T(8,128)(2,1)S(1)} %copy.65), channel_id=1, source_target_pairs={{8,0},{16,8},{24,16},{0,24},{9,1},{17,9},{25,17},{1,25},{10,2},{18... | collective-permute-start | bytes 331784 | tf_op jit(solution)/shard_map/ppermute | solution.py:280
  277.7 11.7 %collective-permute-start.25 = (bf16[96,576]{0,1:T(8,128)(2,1)S(1)}, bf16[96,576]{0,1:T(8,128)(2,1)S(1)}, u32[]{:S(2)}, u32[]{:S(2)}) collective-permute-start(bf16[96,576]{0,1:T(8,128)(2,1)S(1)} %copy.65), channel_id=1, source_target_pairs={{16,0},{24,8},{0,16},{8,24},{17,1},{25,9},{1,17},{9,25},{18,2},{26... | collective-permute-start | bytes 331784 | tf_op jit(solution)/shard_map/ppermute | solution.py:280
  277.7 11.7 %collective-permute-start.26 = (bf16[96,576]{0,1:T(8,128)(2,1)S(1)}, bf16[96,576]{0,1:T(8,128)(2,1)S(1)}, u32[]{:S(2)}, u32[]{:S(2)}) collective-permute-start(bf16[96,576]{0,1:T(8,128)(2,1)S(1)} %copy.65), channel_id=1, source_target_pairs={{24,0},{0,8},{8,16},{16,24},{25,1},{1,9},{9,17},{17,25},{26,2},{2,... | collective-permute-start | bytes 331784 | tf_op jit(solution)/shard_map/ppermute | solution.py:280
  328.0 57.3 %collective-permute-start.30 = (bf16[2,2,96,768]{3,2,1,0:T(8,128)(2,1)S(1)}, bf16[2,2,96,768]{3,2,1,0:T(8,128)(2,1)S(1)}, u32[]{:S(2)}, u32[]{:S(2)}) collective-permute-start(bf16[2,2,96,768]{3,2,1,0:T(8,128)(2,1)S(1)} %slice_bitcast_fusion.2), channel_id=1, source_target_pairs={{0,16},{8,24},{16,0},{24,8},{1,17},{9,25},{17,1},{25,9},{2,18},{10... | collective-permute-start | bytes 1769480 | tf_op jit(solution)/shard_map/ppermute | solution.py:285
  367.2 7.9 %collective-permute-start.27 = (bf16[96,768]{1,0:T(8,128)(2,1)}, bf16[96,768]{1,0:T(8,128)(2,1)}, u32[]{:S(2)}, u32[]{:S(2)}) collective-permute-start(bf16[96,768]{1,0:T(8,128)(2,1)} %reduce-scatter.6.cloned.1.call-done), channel_id=1, source_target_pairs={{8,0},{16,8},{24,16},{0,24},{9,1},{17,9},{25,17},{1,25},{10,2},{18... | collective-permute-start | bytes 442376 | tf_op jit(solution)/shard_map/ppermute | solution.py:280
  370.5 12.9 %collective-permute-start.28 = (bf16[96,768]{1,0:T(8,128)(2,1)}, bf16[96,768]{1,0:T(8,128)(2,1)}, u32[]{:S(2)}, u32[]{:S(2)}) collective-permute-start(bf16[96,768]{1,0:T(8,128)(2,1)} %reduce-scatter.6.cloned.1.call-done), channel_id=1, source_target_pairs={{16,0},{24,8},{0,16},{8,24},{17,1},{25,9},{1,17},{9,25},{18,2},{26... | collective-permute-start | bytes 442376 | tf_op jit(solution)/shard_map/ppermute | solution.py:280
  370.5 12.9 %collective-permute-start.29 = (bf16[96,768]{1,0:T(8,128)(2,1)}, bf16[96,768]{1,0:T(8,128)(2,1)}, u32[]{:S(2)}, u32[]{:S(2)}) collective-permute-start(bf16[96,768]{1,0:T(8,128)(2,1)} %reduce-scatter.6.cloned.1.call-done), channel_id=1, source_target_pairs={{24,0},{0,8},{8,16},{16,24},{25,1},{1,9},{9,17},{17,25},{26,2},{2,... | collective-permute-start | bytes 442376 | tf_op jit(solution)/shard_map/ppermute | solution.py:280
  371.7 13.6 %copy-start.9 = (bf16[1,2,2,2,96,768]{5,4,3,2,1,0:T(8,128)(2,1)S(1)}, bf16[1,2,2,2,96,768]{5,4,3,2,1,0:T(8,128)(2,1)}, u32[]{:S(2)}) copy-start(bf16[1,2,2,2,96,768]{5,4,3,2,1,0:T(8,128)(2,1)} %reduce-scatter.8.cloned.1.call-done) | copy-start | bytes 3538948
  (19 other events, 53.6 us)
Sparse Core Ops, SparseCore 0:
  9.9 26.7 all-gather.4
  40.4 63.6 all-gather.8
  106.6 30.6 all-gather.6
  211.9 34.7 reduce-scatter.9
  250.5 76.4 reduce-scatter.7
  330.4 36.7 reduce-scatter.5
